TPU v7x, 768 devices: a whole 4x8x12 slice. The times are simulated.
768 devices in a mesh: row: 96 (over z, y), col: 8 (over x, core).
Axes of the slice: x: 4, y: 8, z: 12, core: 2. Of those that a mesh axis runs over, the one named last changes fastest.
Arguments:
- pooled_grad: bfloat16 [3072, 8, 512], P(('row', 'col')), may hold values from -6 to 6
- cold_table: float32 [512, 196608], P('col', 'row'), may hold values from -4 to 4
- cold_accum: float32 [196608], P('row'), may hold values from 0.05 to 0.5
- hot_table: float32 [512, 192], P('col'), may hold values from -4 to 4
- hot_accum: float32 [192], replicated, may hold values from 0.05 to 0.5
- cold_owner: int32 [36864, 1], P('row'), may hold values from 0 to 95; in each aligned block of 384 rows (0 to 383, 384 to 767, ...) at most 8 rows name the same one
- cold_row: int32 [36864], P('row'), may hold values from 0 to 2047
- cold_bag: int32 [36864], P('row'), may hold values from 0 to 255
- hot_id: int32 [49152], P('row'), may hold values from 0 to 191
- hot_bag: int32 [49152], P('row'), may hold values from 0 to 255
Outputs:
- new_cold: float32 [512, 196608], P('col', 'row')
- new_cold_accum: float32 [196608], P('row')
- new_hot: float32 [512, 192], P('col')
- new_hot_accum: float32 [192], replicated
Inputs may be any that keep to these rules, and one draw needn't show every extreme that they name: `cold_owner`: within the rows of one device, at most 8 lookups name one owner, and in every draw some owner is named by exactly 8 of them.
All inputs are finite; a program needn't handle non-finite values.
Results may differ from a plain program's by a relative error of at most 0.0003.
Values may be sent and summed in bfloat16 or wider, within the bound.
A program may use at most 32 MiB of HBM per device.

v0:
```python
import jax
import jax.numpy as jnp
from jax import lax
from jax.sharding import PartitionSpec as P

E = 512


LR = 0.3
EPS = 1e-08


def adagrad(table, accum, grad, squares):
    new_accum = accum + squares / E
    new_table = table - LR * grad / (jnp.sqrt(new_accum) + EPS)[None, :]
    return (new_table, new_accum)


def expand(bag_index, bags):
    picker = (bag_index[:, None] == jnp.arange(bags.shape[0], dtype=jnp.int32)[None, :]).astype(
        jnp.bfloat16
    )
    return jnp.dot(picker, bags, preferred_element_type=jnp.float32).astype(jnp.bfloat16)


def contract_lookups(values, placer):
    return lax.dot_general(
        values, placer, (((0,), (0,)), ((), ())), preferred_element_type=jnp.float32
    )


def on_device(
    pooled_grad,
    cold_table,
    cold_accum,
    hot_table,
    hot_accum,
    cold_owner,
    cold_row,
    cold_bag,
    hot_id,
    hot_bag,
):
    num_rows = lax.axis_size("row")
    columns = lax.all_to_all(pooled_grad, "col", split_axis=2, concat_axis=0, tiled=True)
    bags = columns.reshape(-1, columns.shape[2])
    expanded = expand(cold_bag, bags)
    owner = cold_owner[:, 0]
    lookups = owner.shape[0]
    capacity = 2 * lookups // num_rows
    target = (owner[:, None] == jnp.arange(num_rows, dtype=jnp.int32)[None, :]).astype(jnp.int32)
    rank = jnp.sum((jnp.cumsum(target, axis=0) - 1) * target, axis=1)
    slot = owner * capacity + rank
    placed = slot[None, :] == jnp.arange(num_rows * capacity, dtype=jnp.int32)[:, None]
    outgoing = jnp.dot(
        placed.astype(jnp.bfloat16), expanded, preferred_element_type=jnp.float32
    ).astype(jnp.bfloat16)
    out_rows = jnp.sum(jnp.where(placed, cold_row[None, :] + 1, 0), axis=1) - 1
    arrived, arrived_rows = (
        lax.all_to_all(outgoing, "row", split_axis=0, concat_axis=0, tiled=True),
        lax.all_to_all(out_rows, "row", split_axis=0, concat_axis=0, tiled=True),
    )
    local_rows = cold_table.shape[1]
    landing = (arrived_rows[:, None] == jnp.arange(local_rows, dtype=jnp.int32)[None, :]).astype(
        jnp.bfloat16
    )
    cold_grad = contract_lookups(arrived, landing)
    cold_squares = jnp.sum(cold_grad * cold_grad, axis=0)
    hot_expanded = expand(hot_bag, bags)
    hot_count = hot_table.shape[1]
    hot_place = (hot_id[:, None] == jnp.arange(hot_count, dtype=jnp.int32)[None, :]).astype(
        jnp.bfloat16
    )
    hot_partial = contract_lookups(hot_expanded, hot_place)
    hot_grad = lax.psum(hot_partial, "row")
    cold_total, hot_total = lax.psum((cold_squares, jnp.sum(hot_grad * hot_grad, axis=0)), "col")
    new_hot, new_hot_accum = adagrad(hot_table, hot_accum, hot_grad, hot_total)
    new_cold, new_cold_accum = adagrad(cold_table, cold_accum, cold_grad, cold_total)
    return (new_cold, new_cold_accum, new_hot, new_hot_accum)


def solution(mesh):
    in_specs = (
        P(("row", "col"), None, None),
        P("col", "row"),
        P("row"),
        P("col", None),
        P(),
        P("row", None),
        P("row"),
        P("row"),
        P("row"),
        P("row"),
    )
    out_specs = (P("col", "row"), P("row"), P("col", None), P())
    return jax.shard_map(
        on_device, mesh=mesh, in_specs=in_specs, out_specs=out_specs, check_vma=False
    )
```

profile of v0, /device:TPU:1, one launch (start us, length us, event | category | flops | bytes accessed | tf_op | source)
XLA Modules:
  0.0 491.8 jit_solution(78769492742295450)
XLA Ops:
  0.7 0.7 reduce
  1.4 1.0 reduce-window.6
  2.3 0.2 slice_reduce_fusion
  2.6 0.1 fusion.13
  2.8 0.2 select_reduce_fusion
  3.0 0.7 sub.24
  3.7 22.5 %all-to-all-start.2 = ((s32[96,8,1]{1,2,0:T(1,128)}), s32[96,8,1]{1,2,0:T(1,128)S(1)}, u32[]{:S(2)}, u32[]{:S(2)}) async-start(s32[96,8,1]{1,2,0:T(1,128)} %bitcast.6), calls=%async_computation.2 | async-start | bytes 98304 | tf_op jit(solution)/shard_map/all_to_all | solution.py:61
  26.2 0.3 copy.23
  26.6 1.1 reshape.77
  27.7 11.5 %all-to-all-done.2 = s32[96,8,1]{1,2,0:T(1,128)S(1)} async-done(((s32[96,8,1]{1,2,0:T(1,128)}), s32[96,8,1]{1,2,0:T(1,128)S(1)}, u32[]{:S(2)}, u32[]{:S(2)}) %all-to-all-start.2) | async-done | bytes 3104 | tf_op jit(solution)/shard_map/all_to_all | solution.py:61
  39.1 6.4 %all-to-all-start = ((bf16[8,2,1024]{2,1,0:T(2,128)(2,1)}), bf16[8,2,1024]{2,1,0:T(2,128)(2,1)S(1)}, u32[]{:S(2)}, u32[]{:S(2)}) async-start(bf16[8,2,1024]{2,1,0:T(2,128)(2,1)} %reshape.77), calls=%async_computation | async-start | bytes 65536 | tf_op jit(solution)/shard_map/all_to_all | solution.py:45
  45.6 0.5 broadcast.60
  46.1 0.8 reduce.7
  46.9 0.1 eq.103
  46.9 0.0 copy-start.6
  47.0 3.3 all-to-all-done
  50.3 0.6 reshape.78
  50.9 0.2 copy.24
  51.2 0.6 fusion.3
  51.7 0.0 copy-start.8
  51.7 0.2 copy.25
  51.9 0.8 reshape.79
  52.8 5.9 %all-to-all-start.1 = ((bf16[96,2,256]{2,1,0:T(2,128)(2,1)}), bf16[96,2,256]{2,1,0:T(2,128)(2,1)S(1)}, u32[]{:S(2)}, u32[]{:S(2)}) async-start(bf16[96,2,256]{2,1,0:T(2,128)(2,1)} %reshape.79), calls=%async_computation.1 | async-start | bytes 196608 | tf_op jit(solution)/shard_map/all_to_all | solution.py:60
  58.7 0.4 fusion.4
  59.1 333.5 %psum.22 = f32[64,192]{1,0:T(8,128)S(1)} all-reduce(f32[64,192]{1,0:T(8,128)S(1)} %fusion.4), channel_id=1, replica_groups=mesh['row'=96,'col'=8] {'row'}, use_global_device_ids=true, to_apply=%region_6.7 | all-reduce | flops 12288 | bytes 98304 | tf_op jit(solution)/shard_map/psum | solution.py:75
  392.7 0.2 reshape.80
  392.9 1.4 multiply_reduce_fusion
  394.3 94.8 %all-reduce = (f32[2048]{0:T(1024)S(1)}, f32[192]{0:T(256)S(1)}) all-reduce(f32[2048]{0:T(1024)S(1)} %get-tuple-element.10, f32[192]{0:T(256)S(1)} %multiply_reduce_fusion.1), channel_id=1, replica_groups=mesh['row'=96,'col'=8] {'col'}, use_global_device_ids=true, to_apply=%region_5.6 | all-reduce | flops 2240 | bytes 17920 | tf_op jit(solution)/shard_map/psum | solution.py:76
  489.1 0.6 sqrt_add_fusion.1
  489.7 0.6 divide_subtract_fusion.1
  490.3 0.6 sqrt_add_fusion
  490.9 0.9 divide_subtract_fusion
  (22 shorter events, 0.1 us)
Async XLA Ops:
  0.6 2.1 copy-start.4
  0.6 25.6 %copy-start.2 = (bf16[4,8,512]{2,1,0:T(8,128)(2,1)S(1)}, bf16[4,8,512]{2,1,0:T(8,128)(2,1)}, u32[]{:S(2)}) copy-start(bf16[4,8,512]{2,1,0:T(8,128)(2,1)} %param.10) | copy-start | bytes 98308
  3.7 35.5 %all-to-all-start.2 = ((s32[96,8,1]{1,2,0:T(1,128)}), s32[96,8,1]{1,2,0:T(1,128)S(1)}, u32[]{:S(2)}, u32[]{:S(2)}) async-start(s32[96,8,1]{1,2,0:T(1,128)} %bitcast.6), calls=%async_computation.2 | async-start | bytes 98304 | tf_op jit(solution)/shard_map/all_to_all | solution.py:61
  39.1 11.1 %all-to-all-start = ((bf16[8,2,1024]{2,1,0:T(2,128)(2,1)}), bf16[8,2,1024]{2,1,0:T(2,128)(2,1)S(1)}, u32[]{:S(2)}, u32[]{:S(2)}) async-start(bf16[8,2,1024]{2,1,0:T(2,128)(2,1)} %reshape.77), calls=%async_computation | async-start | bytes 65536 | tf_op jit(solution)/shard_map/all_to_all | solution.py:45
  46.9 4.2 copy-start.6
  51.7 7.0 %copy-start.7 = (s32[512]{0:T(512)S(1)}, s32[512]{0:T(512)}, u32[]{:S(2)}) copy-start(s32[512]{0:T(512)} %param.18) | copy-start | bytes 6148
  51.7 7.0 %copy-start.8 = (s32[512]{0:T(512)S(1)}, s32[512]{0:T(512)}, u32[]{:S(2)}) copy-start(s32[512]{0:T(512)} %param.19) | copy-start | bytes 6148
  52.8 339.9 %all-to-all-start.1 = ((bf16[96,2,256]{2,1,0:T(2,128)(2,1)}), bf16[96,2,256]{2,1,0:T(2,128)(2,1)S(1)}, u32[]{:S(2)}, u32[]{:S(2)}) async-start(bf16[96,2,256]{2,1,0:T(2,128)(2,1)} %reshape.79), calls=%async_computation.1 | async-start | bytes 196608 | tf_op jit(solution)/shard_map/all_to_all | solution.py:60
  392.9 96.2 %copy-start.5 = (f32[192]{0:T(256)S(1)}, f32[192]{0:T(256)}, u32[]{:S(2)}) copy-start(f32[192]{0:T(256)} %param.14) | copy-start | bytes 2308
  392.9 96.8 %copy-start.1 = (f32[64,192]{1,0:T(8,128)S(1)}, f32[64,192]{1,0:T(8,128)}, u32[]{:S(2)}) copy-start(f32[64,192]{1,0:T(8,128)} %param.13) | copy-start | bytes 147460
  392.9 97.4 %copy-start.3 = (f32[2048]{0:T(1024)S(1)}, f32[2048]{0:T(1024)}, u32[]{:S(2)}) copy-start(f32[2048]{0:T(1024)} %param.12) | copy-start | bytes 24580
  392.9 98.0 %copy-start = (f32[64,2048]{1,0:T(8,128)S(1)}, f32[64,2048]{1,0:T(8,128)}, u32[]{:S(2)}) copy-start(f32[64,2048]{1,0:T(8,128)} %param.11) | copy-start | bytes 1572868
where the time goes:
time: 492 us
  blocking collectives  428 us (87%)
  starting transfers between devices  34.9 us (7%)
  waiting for transfers between devices  14.8 us (3%)
  other arithmetic  5.53 us (1%)
  local copies, waits for them, and re-layouts  5.04 us (1%)
    psum x1, blocking collectives, on_device(): hot_grad = lax.psum(hot_partial, 'row')  334 us
    psum x1, blocking collectives, on_device(): lax.psum((cold_squares, jnp.sum(hot_grad * hot_grad, axis=0)), 'col')  94.8 us
    all_to_all x1, starting transfers between devices, on_device(): lax.all_to_all(out_rows, 'row', split_axis=0, concat_axis=0, tiled=True)  22.5 us
    all_to_all x1, waiting for transfers between devices, on_device(): lax.all_to_all(out_rows, 'row', split_axis=0, concat_axis=0, tiled=True)  11.5 us
  transfers between devices with their start and end apart: 3, of which 2 were waited for; matrix products, arithmetic and copies ran while one was open for 1% of the time, Pallas kernels for 0%

commit v1 on v0

--- a/solution.py
+++ b/solution.py
@@ -72,7 +72,11 @@
         jnp.bfloat16
     )
     hot_partial = contract_lookups(hot_expanded, hot_place)
-    hot_grad = lax.psum(hot_partial, "row")
+    pieces = lax.all_to_all(hot_partial.T, "row", split_axis=0, concat_axis=0, tiled=True)
+    own_sum = jnp.sum(pieces.reshape(num_rows, hot_count // num_rows, -1), axis=0)
+    spread = jnp.broadcast_to(own_sum[None], (num_rows,) + own_sum.shape)
+    hot_grad = lax.all_to_all(spread, "row", split_axis=0, concat_axis=0, tiled=True)
+    hot_grad = hot_grad.reshape(hot_count, -1).T
     cold_total, hot_total = lax.psum((cold_squares, jnp.sum(hot_grad * hot_grad, axis=0)), "col")
     new_hot, new_hot_accum = adagrad(hot_table, hot_accum, hot_grad, hot_total)
     new_cold, new_cold_accum = adagrad(cold_table, cold_accum, cold_grad, cold_total)

time: 492 us -> 130 us (0.26)
  blocking collectives: 428 us -> 17.8 us
  waiting for transfers between devices: 14.8 us -> 48.1 us
  starting transfers between devices: 34.9 us -> 45.4 us
    psum x1 -> x0, blocking collectives: 334 us -> none  [on_device(): hot_grad = lax.psum(hot_partial, 'row')]
    psum x1, blocking collectives: 94.8 us -> 17.8 us  [on_device(): lax.psum((cold_squares, jnp.sum(hot_grad * hot_grad, axis=0)), 'col')]
    all_to_all x0 -> x2, waiting for transfers between devices: none -> 23.6 us  [the longest x1 12.2 us: on_device(): lax.all_to_all(hot_partial.T, 'row', split_axis=0, concat_axis=0, tiled=T...]
    all_to_all x0 -> x2, starting transfers between devices: none -> 19.7 us  [the longest x1 13.7 us: on_device(): lax.all_to_all(hot_partial.T, 'row', split_axis=0, concat_axis=0, tiled=T...]
    all_to_all x1, starting transfers between devices: 22.5 us -> 5.91 us  [on_device(): lax.all_to_all(out_rows, 'row', split_axis=0, concat_axis=0, tiled=True)]
    all_to_all x1, waiting for transfers between devices: 0.01 us -> 10.8 us  [on_device(): lax.all_to_all(outgoing, 'row', split_axis=0, concat_axis=0, tiled=True)]
    all_to_all x1, starting transfers between devices: 6.42 us -> 13.9 us  [on_device(): lax.all_to_all(pooled_grad, 'col', split_axis=2, concat_axis=0, tiled=True)]
  transfers between devices with their start and end apart: 3 -> 5, of which waited for: 2 -> 5; matrix products, arithmetic and copies ran while one was open for 1% -> 7% of each run, Pallas kernels for 0% -> 0%
where the time goes in v1:
time: 130 us
  waiting for transfers between devices  48.1 us (37%)
  starting transfers between devices  45.4 us (35%)
  blocking collectives  17.8 us (14%)
  local copies, waits for them, and re-layouts  9 us (7%)
  other arithmetic  6.09 us (5%)
  matrix products  2.4 us (2%)
    psum x1, blocking collectives, on_device(): lax.psum((cold_squares, jnp.sum(hot_grad * hot_grad, axis=0)), 'col')  17.8 us
    all_to_all x1, starting transfers between devices, on_device(): lax.all_to_all(pooled_grad, 'col', split_axis=2, concat_axis=0, tiled=True)  13.9 us
    all_to_all x1, starting transfers between devices, on_device(): lax.all_to_all(hot_partial.T, 'row', split_axis=0, concat_axis=0, tiled=T...  13.7 us
    all_to_all x1, waiting for transfers between devices, on_device(): lax.all_to_all(hot_partial.T, 'row', split_axis=0, concat_axis=0, tiled=T...  12.2 us
    all_to_all x1, waiting for transfers between devices, on_device(): lax.all_to_all(spread, 'row', split_axis=0, concat_axis=0, tiled=True)  11.4 us
    all_to_all x1, waiting for transfers between devices, on_device(): lax.all_to_all(outgoing, 'row', split_axis=0, concat_axis=0, tiled=True)  10.8 us
    all_to_all x1, waiting for transfers between devices, on_device(): lax.all_to_all(out_rows, 'row', split_axis=0, concat_axis=0, tiled=True)  10.6 us
    unnamed x29, local copies, waits for them, and re-layouts  6.39 us
  transfers between devices with their start and end apart: 5, of which 5 were waited for; matrix products, arithmetic and copies ran while one was open for 7% of the time, Pallas kernels for 0%

profile of v1, /device:TPU:1, one launch (start us, length us, event | category | flops | bytes accessed | tf_op | source)
XLA Modules:
  0.0 129.8 jit_solution(5451858311026207807)
XLA Ops:
  0.6 1.1 copy.29
  1.7 1.1 reshape.87
  2.8 13.9 %all-to-all-start = ((bf16[8,2,1024]{2,1,0:T(2,128)(2,1)}), bf16[8,2,1024]{2,1,0:T(2,128)(2,1)S(1)}, u32[]{:S(2)}, u32[]{:S(2)}) async-start(bf16[8,2,1024]{2,1,0:T(2,128)(2,1)} %reshape.87), calls=%async_computation | async-start | bytes 65536 | tf_op jit(solution)/shard_map/all_to_all | solution.py:45
  16.8 1.0 reduce-window.6
  18.4 3.1 %all-to-all-done = bf16[8,2,1024]{2,1,0:T(2,128)(2,1)S(1)} async-done(((bf16[8,2,1024]{2,1,0:T(2,128)(2,1)}), bf16[8,2,1024]{2,1,0:T(2,128)(2,1)S(1)}, u32[]{:S(2)}, u32[]{:S(2)}) %all-to-all-start) | async-done | bytes 32800 | tf_op jit(solution)/shard_map/all_to_all | solution.py:45
  21.5 0.6 reshape.88
  22.1 0.2 copy.30
  22.3 0.5 fusion.4
  22.9 0.7 reshape.91
  23.6 13.7 %all-to-all-start.3 = ((f32[96,1,128]{2,1,0:T(1,128)}), f32[96,1,128]{2,1,0:T(1,128)S(1)}, u32[]{:S(2)}, u32[]{:S(2)}) async-start(f32[96,1,128]{2,1,0:T(1,128)} %reshape.91), calls=%async_computation.3 | async-start | bytes 98304 | tf_op jit(solution)/shard_map/all_to_all | solution.py:75
  37.4 0.7 sub.24
  38.1 12.2 %all-to-all-done.3 = f32[96,1,128]{2,1,0:T(1,128)S(1)} async-done(((f32[96,1,128]{2,1,0:T(1,128)}), f32[96,1,128]{2,1,0:T(1,128)S(1)}, u32[]{:S(2)}, u32[]{:S(2)}) %all-to-all-start.3) | async-done | bytes 49184 | tf_op jit(solution)/shard_map/all_to_all | solution.py:75
  50.3 5.9 %all-to-all-start.2 = ((s32[96,8,1]{1,2,0:T(1,128)}), s32[96,8,1]{1,2,0:T(1,128)S(1)}, u32[]{:S(2)}, u32[]{:S(2)}) async-start(s32[96,8,1]{1,2,0:T(1,128)} %bitcast.6), calls=%async_computation.2 | async-start | bytes 98304 | tf_op jit(solution)/shard_map/all_to_all | solution.py:61
  56.2 0.5 broadcast.69
  56.7 0.8 reduce.11
  57.7 0.7 reshape.93
  58.5 10.6 %all-to-all-done.2 = s32[96,8,1]{1,2,0:T(1,128)S(1)} async-done(((s32[96,8,1]{1,2,0:T(1,128)}), s32[96,8,1]{1,2,0:T(1,128)S(1)}, u32[]{:S(2)}, u32[]{:S(2)}) %all-to-all-start.2) | async-done | bytes 3104 | tf_op jit(solution)/shard_map/all_to_all | solution.py:61
  69.1 5.9 %all-to-all-start.4 = ((f32[96,1,128]{2,1,0:T(1,128)}), f32[96,1,128]{2,1,0:T(1,128)S(1)}, u32[]{:S(2)}, u32[]{:S(2)}) async-start(f32[96,1,128]{2,1,0:T(1,128)} %reshape.93), calls=%async_computation.4 | async-start | bytes 98304 | tf_op jit(solution)/shard_map/all_to_all | solution.py:78
  75.0 0.5 fusion.3
  75.8 0.8 reshape.89
  76.6 11.4 %all-to-all-done.4 = f32[96,1,128]{2,1,0:T(1,128)S(1)} async-done(((f32[96,1,128]{2,1,0:T(1,128)}), f32[96,1,128]{2,1,0:T(1,128)S(1)}, u32[]{:S(2)}, u32[]{:S(2)}) %all-to-all-start.4) | async-done | bytes 49184 | tf_op jit(solution)/shard_map/all_to_all | solution.py:78
  88.0 5.9 %all-to-all-start.1 = ((bf16[96,2,256]{2,1,0:T(2,128)(2,1)}), bf16[96,2,256]{2,1,0:T(2,128)(2,1)S(1)}, u32[]{:S(2)}, u32[]{:S(2)}) async-start(bf16[96,2,256]{2,1,0:T(2,128)(2,1)} %reshape.89), calls=%async_computation.1 | async-start | bytes 196608 | tf_op jit(solution)/shard_map/all_to_all | solution.py:60
  94.1 0.5 broadcast.66
  94.6 0.8 reduce.10
  95.5 0.8 reduce.12
  96.7 10.8 %all-to-all-done.1 = bf16[96,2,256]{2,1,0:T(2,128)(2,1)S(1)} async-done(((bf16[96,2,256]{2,1,0:T(2,128)(2,1)}), bf16[96,2,256]{2,1,0:T(2,128)(2,1)S(1)}, u32[]{:S(2)}, u32[]{:S(2)}) %all-to-all-start.1) | async-done | bytes 98336 | tf_op jit(solution)/shard_map/all_to_all | solution.py:60
  107.7 1.4 %multiply_reduce_fusion = (f32[2048]{0:T(1024)S(1)}, f32[64,2048]{1,0:T(8,128)S(1)}) fusion(s32[768]{0:T(1024)S(1)} %eq.103, bf16[96,8,64]{2,1,0:T(8,128)(2,1)S(1)} %reshape.90), kind=kOutput, calls=%fused_computation.14 | convolution fusion | flops 203159552 | bytes 633856 | tf_op jit(solution)/shard_map/dot_general | solution.py:27
  109.1 17.8 %all-reduce = (f32[2048]{0:T(1024)S(1)}, f32[192]{0:T(256)S(1)}) all-reduce(f32[2048]{0:T(1024)S(1)} %get-tuple-element.24, f32[192]{0:T(256)S(1)} %reduce_sum.52), channel_id=1, replica_groups=mesh['row'=96,'col'=8] {'col'}, use_global_device_ids=true, to_apply=%region_5.6 | all-reduce | flops 2240 | bytes 17920 | tf_op jit(solution)/shard_map/psum | solution.py:80
  126.9 0.6 sqrt_add_fusion.1
  127.6 0.7 copy.35
  128.3 0.6 sqrt_add_fusion
  128.9 0.9 divide_subtract_fusion
  (37 shorter events, 2.0 us)
Async XLA Ops:
  0.6 16.1 %copy-start.4 = (s32[384,1]{0,1:T(1,128)S(1)}, s32[384,1]{0,1:T(1,128)}, u32[]{:S(2)}) copy-start(s32[384,1]{0,1:T(1,128)} %param.15) | copy-start | bytes 4612
  2.8 15.3 %copy-start.3 = (s32[384]{0:T(512)S(1)}, s32[384]{0:T(512)}, u32[]{:S(2)}) copy-start(s32[384]{0:T(512)} %param.16) | copy-start | bytes 4612
  2.8 18.6 %all-to-all-start = ((bf16[8,2,1024]{2,1,0:T(2,128)(2,1)}), bf16[8,2,1024]{2,1,0:T(2,128)(2,1)S(1)}, u32[]{:S(2)}, u32[]{:S(2)}) async-start(bf16[8,2,1024]{2,1,0:T(2,128)(2,1)} %reshape.87), calls=%async_computation | async-start | bytes 65536 | tf_op jit(solution)/shard_map/all_to_all | solution.py:45
  18.4 4.0 %copy-start.6 = (s32[512]{0:T(512)S(1)}, s32[512]{0:T(512)}, u32[]{:S(2)}) copy-start(s32[512]{0:T(512)} %param.19) | copy-start | bytes 6148
  18.4 4.0 %copy-start.7 = (s32[512]{0:T(512)S(1)}, s32[512]{0:T(512)}, u32[]{:S(2)}) copy-start(s32[512]{0:T(512)} %param.18) | copy-start | bytes 6148
  22.8 52.2 %copy-start.8 = (s32[384]{0:T(512)S(1)}, s32[384]{0:T(512)}, u32[]{:S(2)}) copy-start(s32[384]{0:T(512)} %param.17) | copy-start | bytes 4612
  23.6 26.7 %all-to-all-start.3 = ((f32[96,1,128]{2,1,0:T(1,128)}), f32[96,1,128]{2,1,0:T(1,128)S(1)}, u32[]{:S(2)}, u32[]{:S(2)}) async-start(f32[96,1,128]{2,1,0:T(1,128)} %reshape.91), calls=%async_computation.3 | async-start | bytes 98304 | tf_op jit(solution)/shard_map/all_to_all | solution.py:75
  50.3 18.8 %all-to-all-start.2 = ((s32[96,8,1]{1,2,0:T(1,128)}), s32[96,8,1]{1,2,0:T(1,128)S(1)}, u32[]{:S(2)}, u32[]{:S(2)}) async-start(s32[96,8,1]{1,2,0:T(1,128)} %bitcast.6), calls=%async_computation.2 | async-start | bytes 98304 | tf_op jit(solution)/shard_map/all_to_all | solution.py:61
  69.1 18.9 %all-to-all-start.4 = ((f32[96,1,128]{2,1,0:T(1,128)}), f32[96,1,128]{2,1,0:T(1,128)S(1)}, u32[]{:S(2)}, u32[]{:S(2)}) async-start(f32[96,1,128]{2,1,0:T(1,128)} %reshape.93), calls=%async_computation.4 | async-start | bytes 98304 | tf_op jit(solution)/shard_map/all_to_all | solution.py:78
  75.6 18.4 %copy-start.1 = (f32[64,192]{1,0:T(8,128)S(1)}, f32[64,192]{1,0:T(8,128)}, u32[]{:S(2)}) copy-start(f32[64,192]{1,0:T(8,128)} %param.13) | copy-start | bytes 147460
  88.0 19.5 %all-to-all-start.1 = ((bf16[96,2,256]{2,1,0:T(2,128)(2,1)}), bf16[96,2,256]{2,1,0:T(2,128)(2,1)S(1)}, u32[]{:S(2)}, u32[]{:S(2)}) async-start(bf16[96,2,256]{2,1,0:T(2,128)(2,1)} %reshape.89), calls=%async_computation.1 | async-start | bytes 196608 | tf_op jit(solution)/shard_map/all_to_all | solution.py:60
  107.7 19.2 %copy-start.5 = (f32[192]{0:T(256)S(1)}, f32[192]{0:T(256)}, u32[]{:S(2)}) copy-start(f32[192]{0:T(256)} %param.14) | copy-start | bytes 2308
  107.7 20.6 %copy-start.2 = (f32[2048]{0:T(1024)S(1)}, f32[2048]{0:T(1024)}, u32[]{:S(2)}) copy-start(f32[2048]{0:T(1024)} %param.12) | copy-start | bytes 24580
  107.7 21.2 %copy-start = (f32[64,2048]{1,0:T(8,128)S(1)}, f32[64,2048]{1,0:T(8,128)}, u32[]{:S(2)}) copy-start(f32[64,2048]{1,0:T(8,128)} %param.11) | copy-start | bytes 1572868

commit v2 on v0

v2 whole, which is shorter than its diff:
```python
import jax
import jax.numpy as jnp
from jax import lax
from jax.experimental import pallas as pl
from jax.experimental.pallas import tpu as pltpu
from jax.sharding import PartitionSpec as P

E = 512
LR = 0.3
EPS = 1e-08
MESH = pl.DeviceIdType.MESH

NC = 8
NY = 8
NZ = 12
LK = 384
LH = 512
CAP = 8
F32 = jnp.float32
BF16 = jnp.bfloat16


def iota(shape, dim):
    return lax.broadcasted_iota(jnp.int32, shape, dim)


def one_hot(mask):
    return jnp.where(mask, 1.0, 0.0).astype(BF16)


def dot(a, b):
    return jnp.dot(a, b, preferred_element_type=F32)


def dot_t(a, b):
    return lax.dot_general(a, b, (((1,), (1,)), ((), ())), preferred_element_type=F32)


def exchange_kernel(
    pool_ref,
    owner_ref,
    row_ref,
    bag_ref,
    hot_id_ref,
    hot_bag_ref,
    grad_ref,
    cold_total_ref,
    hot_grad_ref,
    hot_total_ref,
    bags_send,
    bags_recv,
    rows_y_send,
    rows_y_recv,
    rows_z_send,
    rows_z_recv,
    cold_y_send,
    cold_y_recv,
    cold_z_send,
    cold_z_recv,
    hot_z_send,
    hot_z_recv,
    hot_y_recv,
    hot_all_recv,
    square_recv,
    send_sems,
    recv_sems,
):
    row = lax.axis_index("row")
    col = lax.axis_index("col")
    z = lax.div(row, NY)
    y = lax.rem(row, NY)

    def along_col(k):
        other = lax.rem(col + k, NC)
        return other, {"row": row, "col": other}

    def along_y(k):
        other = lax.rem(y + k, NY)
        return other, {"row": z * NY + other, "col": col}

    def along_z(k):
        other = lax.rem(z + k, NZ)
        return other, {"row": other * NY + y, "col": col}

    def start(stage, count, along, me, send, recv):
        for k in range(1, count):
            other, device = along(k)
            pltpu.make_async_remote_copy(
                src_ref=send.at[me if send is recv else other],
                dst_ref=recv.at[me],
                send_sem=send_sems.at[stage],
                recv_sem=recv_sems.at[stage],
                device_id=device,
                device_id_type=MESH,
            ).start()

    def wait(sem, count, ref):
        part = ref.at[pl.ds(0, count - 1)]
        pltpu.make_async_copy(part, part, sem).wait()

    barrier = pltpu.get_barrier_semaphore()
    for count, along in ((NC, along_col), (NY, along_y), (NZ, along_z)):
        for k in range(1, count):
            pl.semaphore_signal(barrier, inc=1, device_id=along(k)[1], device_id_type=MESH)

    low_lanes = iota((16, 128), 1) < 64
    for pair in range(NC // 2):
        first = pool_ref[0:16, pair * 128 : pair * 128 + 128].astype(F32)
        second = pool_ref[16:32, pair * 128 : pair * 128 + 128].astype(F32)
        bags_send[2 * pair] = jnp.where(low_lanes, first, pltpu.roll(second, 64, 1)).astype(BF16)
        bags_send[2 * pair + 1] = jnp.where(low_lanes, pltpu.roll(first, 64, 1), second).astype(BF16)
    bags_recv[col] = bags_send[col]
    pl.semaphore_wait(barrier, NC + NY + NZ - 3)
    start(0, NC, along_col, col, bags_send, bags_recv)

    owner = owner_ref[...].reshape(1, LK)
    target = iota((NY * NZ, LK), 0) == owner
    earlier = one_hot(iota((LK, LK), 0) < iota((LK, LK), 1))
    before = dot(one_hot(target), earlier)
    rank = jnp.sum(jnp.where(target, before, 0.0), axis=0, keepdims=True).astype(jnp.int32)
    owner_z, owner_y = owner >> 3, owner & 7
    half, quarter = rank >> 2, rank & 3
    table_row = row_ref[...].reshape(1, LK)
    line = owner_y * (2 * NZ) + owner_z * 2 + half
    lane = lax.rem(z, 4) * 32 + y * 4 + quarter
    in_lane = iota((128, LK), 0) == lane
    high = jnp.where(in_lane, (table_row >> 8) + 1, 0).astype(F32).astype(BF16)
    low = jnp.where(in_lane, table_row & 255, 0).astype(F32).astype(BF16)
    in_line = one_hot(iota((NY * NZ * 2, LK), 0) == line)
    codes = dot_t(in_line, high) * 256.0 + dot_t(in_line, low)
    rows_y_send[...] = codes.reshape(NY, 2 * NZ, 128)
    rows_y_recv[y] = rows_y_send[y]
    start(1, NY, along_y, y, rows_y_send, rows_y_recv)

    def place_of_bag(bag):
        return ((bag >> 4) & 1) * 128 + (bag >> 5) * 16 + (bag & 15)

    position = owner_y * (NZ * 4) + owner_z * 4 + quarter + half * LK
    placed = one_hot(iota((2 * LK, LK), 0) == position)
    cold_place = place_of_bag(bag_ref[...].reshape(1, LK)) + 1
    cold_place = jnp.broadcast_to(cold_place, (8, LK)).astype(F32).astype(BF16)
    slot_place = dot_t(placed, cold_place)[:, 0:1].astype(jnp.int32)
    bag_number = iota((LK, 256), 1) + 1
    pick = jnp.concatenate(
        [one_hot(slot_place[:LK] == bag_number), one_hot(slot_place[LK:] == bag_number)], axis=1
    )

    hot_id = hot_id_ref[...].reshape(1, LH)
    hot_line = (hot_id >> 4) * 8 + (hot_id & 7) + ((hot_id >> 3) & 1) * (NZ * 8)
    hot_rows = one_hot(iota((NZ * 16, LH), 0) == hot_line)
    hot_place = place_of_bag(hot_bag_ref[...].reshape(1, LH))
    counts = dot_t(hot_rows, one_hot(iota((256, LH), 0) == hot_place))
    counts = jnp.concatenate([counts[: NZ * 8], counts[NZ * 8 :]], axis=1)
    count_high = counts.astype(BF16)
    count_low = (counts - count_high.astype(F32)).astype(BF16)

    wait(recv_sems.at[0], NC, bags_recv)
    bags = bags_recv[...].reshape(128, 128).astype(F32)
    rolled = pltpu.roll(bags, 64, 1)
    left = iota((128, 128), 1) < 64
    spread = jnp.concatenate(
        [
            jnp.where(left, bags, 0.0),
            jnp.where(left, rolled, 0.0),
            jnp.where(left, 0.0, rolled),
            jnp.where(left, 0.0, bags),
        ],
        axis=0,
    ).astype(BF16)
    cold_y_send[...] = dot(pick, spread).astype(BF16).reshape(NY, NZ * 4, 128)
    cold_y_recv[y] = cold_y_send[y]
    start(2, NY, along_y, y, cold_y_send, cold_y_recv)
    hot_z_send[...] = (dot(count_high, spread) + dot(count_low, spread)).reshape(NZ, 8, 128)
    hot_z_recv[z] = hot_z_send[z]
    start(3, NZ, along_z, z, hot_z_send, hot_z_recv)

    wait(recv_sems.at[1], NY, rows_y_recv)
    merged = jnp.sum(rows_y_recv[...], axis=0)
    for other in range(NZ):
        rows_z_send[other, 0:2] = merged[2 * other : 2 * other + 2]
        rows_z_send[other, 2:8] = jnp.zeros((6, 128), F32)
    rows_z_recv[z] = rows_z_send[z]
    start(4, NZ, along_z, z, rows_z_send, rows_z_recv)

    out_row = iota((LK, LK), 0)
    source = ((out_row >> 2) & 7) * (NZ * 4) + (out_row >> 5) * 4 + (out_row & 3)
    regroup = one_hot(iota((LK, LK), 1) == source)

    wait(recv_sems.at[2], NY, cold_y_recv)
    regrouped = dot(regroup, cold_y_recv[...].reshape(LK, 128)).astype(BF16)
    cold_z_send[...] = regrouped.reshape(NZ, 32, 128)
    cold_z_recv[z] = cold_z_send[z]
    start(5, NZ, along_z, z, cold_z_send, cold_z_recv)

    wait(recv_sems.at[3], NZ, hot_z_recv)
    hot_y_recv[y] = jnp.sum(hot_z_recv[...], axis=0)
    start(6, NY, along_y, y, hot_y_recv, hot_y_recv)

    wait(recv_sems.at[4], NZ, rows_z_recv)
    code = jnp.concatenate(
        [jnp.sum(rows_z_recv[4 * g : 4 * g + 4], axis=0) for g in range(NZ // 4)], axis=1
    ).astype(jnp.int32)
    code_high, code_low = code >> 8, code & 255
    low_number = iota((256, LK), 0)
    land = [one_hot(code_low[side : side + 1] == low_number) for side in range(2)]

    wait(recv_sems.at[6], NY, hot_y_recv)
    hot_all_recv[z] = jnp.sum(hot_y_recv[...], axis=0)
    start(7, NZ, along_z, z, hot_all_recv, hot_all_recv)

    wait(recv_sems.at[5], NZ, cold_z_recv)
    arrived = cold_z_recv[...].reshape(LK, 128).astype(F32).T
    grads = jnp.zeros((512, 256), F32)
    for side in range(2):
        mine = arrived[64 * side : 64 * side + 64]
        masked = jnp.concatenate(
            [jnp.where(code_high[side : side + 1] == h + 1, mine, 0.0) for h in range(8)], axis=0
        ).astype(BF16)
        grads += dot_t(masked, land[side])
    squares = []
    for h in range(8):
        part = grads[64 * h : 64 * h + 64]
        grad_ref[:, 256 * h : 256 * h + 256] = part
        squares.append(jnp.sum(part * part, axis=0, keepdims=True))
    square_recv[col, :, 0:256] = jnp.concatenate(squares, axis=0)

    wait(recv_sems.at[7], NZ, hot_all_recv)
    pieces = []
    for other in range(NZ):
        piece = hot_all_recv[other]
        pieces += [piece, pltpu.roll(piece, 64, 1)]
    hot_grad = jnp.concatenate(pieces + [jnp.zeros((64, 128), F32)], axis=0).T[0:64]
    hot_grad_ref[...] = hot_grad
    hot_squares = jnp.sum(hot_grad * hot_grad, axis=0, keepdims=True)
    square_recv[col, :, 256:384] = jnp.concatenate(
        [hot_squares[:, 0:128], hot_squares[:, 128:256], jnp.zeros((6, 128), F32)], axis=0
    )
    start(8, NC, along_col, col, square_recv, square_recv)
    wait(recv_sems.at[8], NC, square_recv)
    total = square_recv[0]
    for other in range(1, NC):
        total += square_recv[other]
    cold_total_ref[...] = total[:, 0:256]
    hot_total_ref[...] = total[:, 256:384]

    for stage, count, send in (
        (0, NC, bags_send),
        (1, NY, rows_y_send),
        (2, NY, cold_y_send),
        (3, NZ, hot_z_send),
        (4, NZ, rows_z_send),
        (5, NZ, cold_z_send),
        (6, NY, hot_y_recv),
        (7, NZ, hot_all_recv),
        (8, NC, square_recv),
    ):
        wait(send_sems.at[stage], count, send)


def exchange(pool, owner, cold_row, cold_bag, hot_id, hot_bag):
    vmem = pl.BlockSpec(memory_space=pltpu.VMEM)
    return pl.pallas_call(
        exchange_kernel,
        out_shape=(
            jax.ShapeDtypeStruct((64, 2048), F32),
            jax.ShapeDtypeStruct((8, 256), F32),
            jax.ShapeDtypeStruct((64, 256), F32),
            jax.ShapeDtypeStruct((8, 128), F32),
        ),
        in_specs=[vmem] * 6,
        out_specs=(vmem,) * 4,
        scratch_shapes=[
            pltpu.VMEM((NC, 16, 128), BF16),
            pltpu.VMEM((NC, 16, 128), BF16),
            pltpu.VMEM((NY, 2 * NZ, 128), F32),
            pltpu.VMEM((NY, 2 * NZ, 128), F32),
            pltpu.VMEM((NZ, 8, 128), F32),
            pltpu.VMEM((NZ, 8, 128), F32),
            pltpu.VMEM((NY, NZ * 4, 128), BF16),
            pltpu.VMEM((NY, NZ * 4, 128), BF16),
            pltpu.VMEM((NZ, 32, 128), BF16),
            pltpu.VMEM((NZ, 32, 128), BF16),
            pltpu.VMEM((NZ, 8, 128), F32),
            pltpu.VMEM((NZ, 8, 128), F32),
            pltpu.VMEM((NY, 8, 128), F32),
            pltpu.VMEM((NZ, 8, 128), F32),
            pltpu.VMEM((NC, 8, 384), F32),
            pltpu.SemaphoreType.DMA((9,)),
            pltpu.SemaphoreType.DMA((9,)),
        ],
        compiler_params=pltpu.CompilerParams(
            collective_id=0, has_side_effects=True, vmem_limit_bytes=32 * 1024 * 1024
        ),
        name="exchange",
    )(pool, owner, cold_row, cold_bag, hot_id, hot_bag)


def update_kernel(
    table_ref,
    accum_ref,
    grad_ref,
    total_ref,
    hot_table_ref,
    hot_accum_ref,
    hot_grad_ref,
    hot_total_ref,
    new_ref,
    new_accum_ref,
    new_hot_ref,
    new_hot_accum_ref,
):
    for h in range(8):
        at = slice(256 * h, 256 * h + 256)
        accum = accum_ref[at].reshape(1, 256) + total_ref[h : h + 1, :] / E
        new_accum_ref[at] = accum.reshape(256)
        scale = LR / (jnp.sqrt(accum) + EPS)
        new_ref[:, at] = table_ref[:, at] - grad_ref[:, at] * scale
    hot_total = jnp.concatenate([hot_total_ref[0:1, :], hot_total_ref[1:2, 0:64]], axis=1)
    accum = hot_accum_ref[...].reshape(1, 192) + hot_total / E
    new_hot_accum_ref[...] = accum.reshape(192)
    new_hot_ref[...] = hot_table_ref[...] - hot_grad_ref[:, 0:192] * (
        LR / (jnp.sqrt(accum) + EPS)
    )


def update(table, accum, grad, total, hot_table, hot_accum, hot_grad, hot_total):
    vmem = pl.BlockSpec(memory_space=pltpu.VMEM)
    return pl.pallas_call(
        update_kernel,
        out_shape=(
            jax.ShapeDtypeStruct(table.shape, F32),
            jax.ShapeDtypeStruct(accum.shape, F32),
            jax.ShapeDtypeStruct(hot_table.shape, F32),
            jax.ShapeDtypeStruct(hot_accum.shape, F32),
        ),
        in_specs=[vmem] * 8,
        out_specs=(vmem,) * 4,
        compiler_params=pltpu.CompilerParams(vmem_limit_bytes=16 * 1024 * 1024),
        name="update",
    )(table, accum, grad, total, hot_table, hot_accum, hot_grad, hot_total)


def on_device(
    pooled_grad,
    cold_table,
    cold_accum,
    hot_table,
    hot_accum,
    cold_owner,
    cold_row,
    cold_bag,
    hot_id,
    hot_bag,
):
    grad, total, hot_grad, hot_total = exchange(
        pooled_grad.reshape(32, E), cold_owner.T, cold_row, cold_bag, hot_id, hot_bag
    )
    return tuple(
        update(cold_table, cold_accum, grad, total, hot_table, hot_accum, hot_grad, hot_total)
    )


def solution(mesh):
    in_specs = (
        P(("row", "col"), None, None),
        P("col", "row"),
        P("row"),
        P("col", None),
        P(),
        P("row", None),
        P("row"),
        P("row"),
        P("row"),
        P("row"),
    )
    out_specs = (P("col", "row"), P("row"), P("col", None), P())
    return jax.shard_map(
        on_device, mesh=mesh, in_specs=in_specs, out_specs=out_specs, check_vma=False
    )
```

time: 492 us -> 53.4 us (0.11)
  blocking collectives: 428 us -> 0 us
  Pallas kernels: 0 us -> 46.3 us
  starting transfers between devices: 34.9 us -> 0 us
  waiting for transfers between devices: 14.8 us -> 0 us
  other arithmetic: 5.53 us -> 0 us
    psum x2 -> x0, blocking collectives: 428 us -> none  [the longest x1 334 us: on_device(): hot_grad = lax.psum(hot_partial, 'row')]
    pallas_call x0 -> x2, Pallas kernels: none -> 46.3 us  [the longest x1 45.4 us: exchange(): pl.pallas_call(exchange_kernel, out_shape=(jax.ShapeDtypeStruct((64, 2048...]
    all_to_all x3 -> x0, starting transfers between devices: 34.9 us -> none  [the longest x1 22.5 us: on_device(): lax.all_to_all(out_rows, 'row', split_axis=0, concat_axis=0, tiled=True)]
    all_to_all x3 -> x0, waiting for transfers between devices: 14.8 us -> none  [the longest x1 11.5 us: on_device(): lax.all_to_all(out_rows, 'row', split_axis=0, concat_axis=0, tiled=True)]
  transfers between devices with their start and end apart: 3 -> 0, of which waited for: 2 -> 0; matrix products, arithmetic and copies ran while one was open for 1% -> 0% of each run, Pallas kernels for 0% -> 0%
where the time goes in v2:
time: 53.4 us; the launch traced here: 53 us
  Pallas kernels  46.3 us (87%)
  local copies, waits for them, and re-layouts  6.03 us (11%)
  between operations  0.68 us (1%)
    pallas_call x1, Pallas kernels, exchange(): pl.pallas_call(exchange_kernel, out_shape=(jax.ShapeDtypeStruct((64, 2048...  45.4 us
    unnamed x20, local copies, waits for them, and re-layouts  6.03 us

profile of v2, /device:TPU:1, one launch (start us, length us, event | category | flops | bytes accessed | tf_op | source)
XLA Modules:
  0.0 53.0 jit_solution(2290099949066558026)
XLA Ops:
  0.6 0.0 copy-start.4
  0.6 0.0 copy-start.8
  0.7 0.7 %copy-done.4 = s32[384]{0:T(512)S(1)} copy-done((s32[384]{0:T(512)S(1)}, s32[384]{0:T(512)}, u32[]{:S(2)}) %copy-start.4) | copy-done | bytes 1560
  1.3 0.0 copy-done.8
  1.3 0.0 copy-start.2
  1.3 0.8 %copy-done.2 = bf16[4,8,512]{2,1,0:T(8,128)(2,1)S(1)} copy-done((bf16[4,8,512]{2,1,0:T(8,128)(2,1)S(1)}, bf16[4,8,512]{2,1,0:T(8,128)(2,1)}, u32[]{:S(2)}) %copy-start.2) | copy-done | bytes 32792
  2.1 0.0 copy-start.5
  2.1 0.7 %copy-done.5 = s32[384]{0:T(512)S(1)} copy-done((s32[384]{0:T(512)S(1)}, s32[384]{0:T(512)}, u32[]{:S(2)}) %copy-start.5) | copy-done | bytes 1560
  2.8 0.0 copy-start.6
  2.8 0.7 %copy-done.6 = s32[512]{0:T(512)S(1)} copy-done((s32[512]{0:T(512)S(1)}, s32[512]{0:T(512)}, u32[]{:S(2)}) %copy-start.6) | copy-done | bytes 2072
  3.5 0.0 copy-start.7
  3.5 0.7 %copy-done.7 = s32[512]{0:T(512)S(1)} copy-done((s32[512]{0:T(512)S(1)}, s32[512]{0:T(512)}, u32[]{:S(2)}) %copy-start.7) | copy-done | bytes 2072
  4.1 0.0 copy-start.3
  4.1 45.4 %exchange.1 = (f32[64,2048]{1,0:T(8,128)S(1)}, f32[8,256]{1,0:T(8,128)S(1)}, f32[64,256]{1,0:T(8,128)S(1)}, f32[8,128]{1,0:T(8,128)S(1)}) custom-call(bf16[32,512]{1,0:T(8,128)(2,1)S(1)} %bitcast.2, s32[1,384]{1,0:T(1,128)S(1)} %bitcast.3, s32[384]{0:T(512)S(1)} %copy-done.4, s32[384]{0:T(512)S(1)} %copy-done.5, s32[512]{0:T(512)S(1)} %copy-done.6, ...), custom_call_target="tpu_custom_call" | custom-call | tf_op jit(solution)/shard_map/exchange/pallas_call | solution.py:262
  49.6 0.0 copy-start.9
  49.6 0.0 copy-done.3
  49.6 0.7 %copy-done.9 = f32[192]{0:T(256)S(1)} copy-done((f32[192]{0:T(256)S(1)}, f32[192]{0:T(256)}, u32[]{:S(2)}) %copy-start.9) | copy-done | bytes 792
  50.2 0.0 copy-start
  50.2 1.0 %copy-done = f32[64,2048]{1,0:T(8,128)S(1)} copy-done((f32[64,2048]{1,0:T(8,128)S(1)}, f32[64,2048]{1,0:T(8,128)}, u32[]{:S(2)}) %copy-start) | copy-done | bytes 524312
  51.3 0.0 copy-start.1
  51.3 0.8 %copy-done.1 = f32[64,192]{1,0:T(8,128)S(1)} copy-done((f32[64,192]{1,0:T(8,128)S(1)}, f32[64,192]{1,0:T(8,128)}, u32[]{:S(2)}) %copy-start.1) | copy-done | bytes 49176
  52.1 0.9 %update.1 = (f32[64,2048]{1,0:T(8,128)}, f32[2048]{0:T(1024)}, f32[64,192]{1,0:T(8,128)}, f32[192]{0:T(256)}) custom-call(f32[64,2048]{1,0:T(8,128)S(1)} %copy-done, f32[2048]{0:T(1024)S(1)} %copy-done.3, f32[64,2048]{1,0:T(8,128)S(1)} %get-tuple-element.8.grad_ref, f32[8,256]{1,0:T(8,128)S(1)} %get-tuple-element.9.total_ref, f32[64,192]{1,0:T(8,128)S(1)} %copy-done.1, ...), custom_call_target="tpu_custom_call" | custom-call | tf_op jit(solution)/shard_map/update/pallas_call | solution.py:328
Async XLA Ops:
  0.6 0.7 %copy-start.4 = (s32[384]{0:T(512)S(1)}, s32[384]{0:T(512)}, u32[]{:S(2)}) copy-start(s32[384]{0:T(512)} %row_ref.1) | copy-start | bytes 4612
  0.6 0.7 %copy-start.8 = (s32[384,1]{0,1:T(1,128)S(1)}, s32[384,1]{0,1:T(1,128)}, u32[]{:S(2)}) copy-start(s32[384,1]{0,1:T(1,128)} %param.15) | copy-start | bytes 4612
  1.3 0.8 %copy-start.2 = (bf16[4,8,512]{2,1,0:T(8,128)(2,1)S(1)}, bf16[4,8,512]{2,1,0:T(8,128)(2,1)}, u32[]{:S(2)}) copy-start(bf16[4,8,512]{2,1,0:T(8,128)(2,1)} %param.10) | copy-start | bytes 98308
  2.1 0.7 %copy-start.5 = (s32[384]{0:T(512)S(1)}, s32[384]{0:T(512)}, u32[]{:S(2)}) copy-start(s32[384]{0:T(512)} %bag_ref.1) | copy-start | bytes 4612
  2.8 0.7 %copy-start.6 = (s32[512]{0:T(512)S(1)}, s32[512]{0:T(512)}, u32[]{:S(2)}) copy-start(s32[512]{0:T(512)} %hot_id_ref.1) | copy-start | bytes 6148
  3.5 0.7 %copy-start.7 = (s32[512]{0:T(512)S(1)}, s32[512]{0:T(512)}, u32[]{:S(2)}) copy-start(s32[512]{0:T(512)} %hot_bag_ref.1) | copy-start | bytes 6148
  4.1 45.4 %copy-start.3 = (f32[2048]{0:T(1024)S(1)}, f32[2048]{0:T(1024)}, u32[]{:S(2)}) copy-start(f32[2048]{0:T(1024)} %accum_ref.1) | copy-start | bytes 24580
  49.6 0.7 %copy-start.9 = (f32[192]{0:T(256)S(1)}, f32[192]{0:T(256)}, u32[]{:S(2)}) copy-start(f32[192]{0:T(256)} %hot_accum_ref.1) | copy-start | bytes 2308
  50.2 1.0 %copy-start = (f32[64,2048]{1,0:T(8,128)S(1)}, f32[64,2048]{1,0:T(8,128)}, u32[]{:S(2)}) copy-start(f32[64,2048]{1,0:T(8,128)} %table_ref.1) | copy-start | bytes 1572868
  51.3 0.8 %copy-start.1 = (f32[64,192]{1,0:T(8,128)S(1)}, f32[64,192]{1,0:T(8,128)}, u32[]{:S(2)}) copy-start(f32[64,192]{1,0:T(8,128)} %hot_table_ref.1) | copy-start | bytes 147460

commit v3 on v2

--- a/solution.py
+++ b/solution.py
@@ -37,16 +37,35 @@
 
 
 def exchange_kernel(
+    pool_hbm,
+    owner_hbm,
+    row_hbm,
+    bag_hbm,
+    hot_id_hbm,
+    hot_bag_hbm,
+    table_hbm,
+    accum_hbm,
+    hot_table_hbm,
+    hot_accum_hbm,
+    new_hbm,
+    new_accum_hbm,
+    new_hot_hbm,
+    new_hot_accum_hbm,
     pool_ref,
     owner_ref,
     row_ref,
     bag_ref,
     hot_id_ref,
     hot_bag_ref,
+    table_ref,
+    accum_ref,
+    hot_table_ref,
+    hot_accum_ref,
+    new_ref,
+    new_accum_ref,
+    new_hot_ref,
+    new_hot_accum_ref,
     grad_ref,
-    cold_total_ref,
-    hot_grad_ref,
-    hot_total_ref,
     bags_send,
     bags_recv,
     rows_y_send,
@@ -62,6 +81,8 @@
     hot_y_recv,
     hot_all_recv,
     square_recv,
+    fetch_sems,
+    store_sems,
     send_sems,
     recv_sems,
 ):
@@ -103,6 +124,27 @@
         for k in range(1, count):
             pl.semaphore_signal(barrier, inc=1, device_id=along(k)[1], device_id_type=MESH)
 
+    fetches = [
+        pltpu.make_async_copy(source, target, fetch_sems.at[i])
+        for i, (source, target) in enumerate(
+            (
+                (pool_hbm, pool_ref),
+                (owner_hbm, owner_ref),
+                (row_hbm, row_ref),
+                (bag_hbm, bag_ref),
+                (hot_id_hbm, hot_id_ref),
+                (hot_bag_hbm, hot_bag_ref),
+                (table_hbm, table_ref),
+                (accum_hbm, accum_ref),
+                (hot_table_hbm, hot_table_ref),
+                (hot_accum_hbm, hot_accum_ref),
+            )
+        )
+    ]
+    for fetch in fetches:
+        fetch.start()
+    fetches[0].wait()
+
     low_lanes = iota((16, 128), 1) < 64
     for pair in range(NC // 2):
         first = pool_ref[0:16, pair * 128 : pair * 128 + 128].astype(F32)
@@ -113,6 +155,8 @@
     pl.semaphore_wait(barrier, NC + NY + NZ - 3)
     start(0, NC, along_col, col, bags_send, bags_recv)
 
+    for fetch in fetches[1:6]:
+        fetch.wait()
     owner = owner_ref[...].reshape(1, LK)
     target = iota((NY * NZ, LK), 0) == owner
     earlier = one_hot(iota((LK, LK), 0) < iota((LK, LK), 1))
@@ -230,18 +274,40 @@
         piece = hot_all_recv[other]
         pieces += [piece, pltpu.roll(piece, 64, 1)]
     hot_grad = jnp.concatenate(pieces + [jnp.zeros((64, 128), F32)], axis=0).T[0:64]
-    hot_grad_ref[...] = hot_grad
     hot_squares = jnp.sum(hot_grad * hot_grad, axis=0, keepdims=True)
     square_recv[col, :, 256:384] = jnp.concatenate(
         [hot_squares[:, 0:128], hot_squares[:, 128:256], jnp.zeros((6, 128), F32)], axis=0
     )
     start(8, NC, along_col, col, square_recv, square_recv)
+    for fetch in fetches[6:]:
+        fetch.wait()
     wait(recv_sems.at[8], NC, square_recv)
     total = square_recv[0]
     for other in range(1, NC):
         total += square_recv[other]
-    cold_total_ref[...] = total[:, 0:256]
-    hot_total_ref[...] = total[:, 256:384]
+    stores = []
+
+    def store(source, target):
+        copy = pltpu.make_async_copy(source, target, store_sems.at[len(stores)])
+        copy.start()
+        stores.append(copy)
+
+    hot_total = jnp.concatenate([total[0:1, 256:384], total[1:2, 256:320]], axis=1)
+    accum = hot_accum_ref[...].reshape(1, 192) + hot_total / E
+    new_hot_accum_ref[...] = accum.reshape(192)
+    store(new_hot_accum_ref, new_hot_accum_hbm)
+    new_hot_ref[...] = hot_table_ref[...] - hot_grad[:, 0:192] * (LR / (jnp.sqrt(accum) + EPS))
+    store(new_hot_ref, new_hot_hbm)
+    for h in range(8):
+        at = slice(256 * h, 256 * h + 256)
+        accum = accum_ref[at].reshape(1, 256) + total[h : h + 1, 0:256] / E
+        new_accum_ref[at] = accum.reshape(256)
+        scale = LR / (jnp.sqrt(accum) + EPS)
+        new_ref[:, at] = table_ref[:, at] - grad_ref[:, at] * scale
+        if h % 2 == 1:
+            done = slice(256 * h - 256, 256 * h + 256)
+            store(new_ref.at[:, done], new_hbm.at[:, done])
+    store(new_accum_ref, new_accum_hbm)
 
     for stage, count, send in (
         (0, NC, bags_send),
@@ -255,21 +321,21 @@
         (8, NC, square_recv),
     ):
         wait(send_sems.at[stage], count, send)
-
-
-def exchange(pool, owner, cold_row, cold_bag, hot_id, hot_bag):
-    vmem = pl.BlockSpec(memory_space=pltpu.VMEM)
+    for copy in stores:
+        copy.wait()
+
+
+def exchange(*operands):
+    hbm = pl.BlockSpec(memory_space=pltpu.HBM)
     return pl.pallas_call(
         exchange_kernel,
-        out_shape=(
-            jax.ShapeDtypeStruct((64, 2048), F32),
-            jax.ShapeDtypeStruct((8, 256), F32),
-            jax.ShapeDtypeStruct((64, 256), F32),
-            jax.ShapeDtypeStruct((8, 128), F32),
-        ),
-        in_specs=[vmem] * 6,
-        out_specs=(vmem,) * 4,
+        out_shape=tuple(jax.ShapeDtypeStruct(a.shape, F32) for a in operands[6:]),
+        in_specs=[hbm] * 10,
+        out_specs=(hbm,) * 4,
         scratch_shapes=[
+            *(pltpu.VMEM(a.shape, a.dtype) for a in operands),
+            *(pltpu.VMEM(a.shape, F32) for a in operands[6:]),
+            pltpu.VMEM((64, 2048), F32),
             pltpu.VMEM((NC, 16, 128), BF16),
             pltpu.VMEM((NC, 16, 128), BF16),
             pltpu.VMEM((NY, 2 * NZ, 128), F32),
@@ -285,59 +351,45 @@
             pltpu.VMEM((NY, 8, 128), F32),
             pltpu.VMEM((NZ, 8, 128), F32),
             pltpu.VMEM((NC, 8, 384), F32),
+            pltpu.SemaphoreType.DMA((10,)),
+            pltpu.SemaphoreType.DMA((7,)),
             pltpu.SemaphoreType.DMA((9,)),
             pltpu.SemaphoreType.DMA((9,)),
         ],
         compiler_params=pltpu.CompilerParams(
-            collective_id=0, has_side_effects=True, vmem_limit_bytes=32 * 1024 * 1024
+            collective_id=0, has_side_effects=True, vmem_limit_bytes=60 * 1024 * 1024
         ),
         name="exchange",
-    )(pool, owner, cold_row, cold_bag, hot_id, hot_bag)
-
-
-def update_kernel(
-    table_ref,
-    accum_ref,
-    grad_ref,
-    total_ref,
-    hot_table_ref,
-    hot_accum_ref,
-    hot_grad_ref,
-    hot_total_ref,
-    new_ref,
-    new_accum_ref,
-    new_hot_ref,
-    new_hot_accum_ref,
-):
-    for h in range(8):
-        at = slice(256 * h, 256 * h + 256)
-        accum = accum_ref[at].reshape(1, 256) + total_ref[h : h + 1, :] / E
-        new_accum_ref[at] = accum.reshape(256)
-        scale = LR / (jnp.sqrt(accum) + EPS)
-        new_ref[:, at] = table_ref[:, at] - grad_ref[:, at] * scale
-    hot_total = jnp.concatenate([hot_total_ref[0:1, :], hot_total_ref[1:2, 0:64]], axis=1)
-    accum = hot_accum_ref[...].reshape(1, 192) + hot_total / E
-    new_hot_accum_ref[...] = accum.reshape(192)
-    new_hot_ref[...] = hot_table_ref[...] - hot_grad_ref[:, 0:192] * (
-        LR / (jnp.sqrt(accum) + EPS)
-    )
-
-
-def update(table, accum, grad, total, hot_table, hot_accum, hot_grad, hot_total):
-    vmem = pl.BlockSpec(memory_space=pltpu.VMEM)
+    )(*operands)
+
+
+def write_kernel(table, accum, hot_table, hot_accum, *refs):
+    sems = refs[4]
+    copies = [
+        (table.at[0:32], refs[0].at[0:32]),
+        (table.at[32:64], refs[0].at[32:64]),
+        (accum, refs[1]),
+        (hot_table, refs[2]),
+        (hot_accum, refs[3]),
+    ]
+    copies = [pltpu.make_async_copy(*pair, sems.at[i]) for i, pair in enumerate(copies)]
+    for copy in copies:
+        copy.start()
+    for copy in copies:
+        copy.wait()
+
+
+def write(*arrays):
+    hbm = pl.BlockSpec(memory_space=pltpu.HBM)
     return pl.pallas_call(
-        update_kernel,
-        out_shape=(
-            jax.ShapeDtypeStruct(table.shape, F32),
-            jax.ShapeDtypeStruct(accum.shape, F32),
-            jax.ShapeDtypeStruct(hot_table.shape, F32),
-            jax.ShapeDtypeStruct(hot_accum.shape, F32),
-        ),
-        in_specs=[vmem] * 8,
-        out_specs=(vmem,) * 4,
-        compiler_params=pltpu.CompilerParams(vmem_limit_bytes=16 * 1024 * 1024),
-        name="update",
-    )(table, accum, grad, total, hot_table, hot_accum, hot_grad, hot_total)
+        write_kernel,
+        out_shape=tuple(jax.ShapeDtypeStruct(a.shape, a.dtype) for a in arrays),
+        in_specs=[hbm] * 4,
+        out_specs=(hbm,) * 4,
+        scratch_shapes=[pltpu.SemaphoreType.DMA((5,))],
+        compiler_params=pltpu.CompilerParams(vmem_limit_bytes=60 * 1024 * 1024),
+        name="write",
+    )(*arrays)
 
 
 def on_device(
@@ -352,12 +404,19 @@
     hot_id,
     hot_bag,
 ):
-    grad, total, hot_grad, hot_total = exchange(
-        pooled_grad.reshape(32, E), cold_owner.T, cold_row, cold_bag, hot_id, hot_bag
+    updated = exchange(
+        pooled_grad.reshape(32, E),
+        cold_owner.T,
+        cold_row,
+        cold_bag,
+        hot_id,
+        hot_bag,
+        cold_table,
+        cold_accum,
+        hot_table,
+        hot_accum,
     )
-    return tuple(
-        update(cold_table, cold_accum, grad, total, hot_table, hot_accum, hot_grad, hot_total)
-    )
+    return tuple(write(*updated))
 
 
 def solution(mesh):

time: 53.4 us -> 66.4 us (1.24)
  Pallas kernels: 46.3 us -> 65.6 us
  local copies, waits for them, and re-layouts: 6.03 us -> 0 us
    pallas_call x2, Pallas kernels: 46.3 us -> 65.6 us  [the longest x1 46.3 us: exchange(): pl.pallas_call(exchange_kernel, out_shape=tuple((jax.ShapeDtypeStruct(a.s...]
    unnamed x20 -> x0, local copies, waits for them, and re-layouts: 6.03 us -> none
where the time goes in v3:
time: 66.4 us; the launch traced here: 66.2 us
  Pallas kernels  65.6 us (99%)
    pallas_call x1, Pallas kernels, exchange(): pl.pallas_call(exchange_kernel, out_shape=tuple((jax.ShapeDtypeStruct(a.s...  46.3 us
    pallas_call x1, Pallas kernels, write(): pl.pallas_call(write_kernel, out_shape=tuple((jax.ShapeDtypeStruct(a.shap...  19.3 us

profile of v3, /device:TPU:1, one launch (start us, length us, event | category | flops | bytes accessed | tf_op | source)
XLA Modules:
  0.0 66.2 jit_solution(13319480221900488574)
XLA Ops:
  0.6 46.3 %exchange.1 = (f32[64,2048]{1,0:T(8,128)}, f32[2048]{0:T(1024)}, f32[64,192]{1,0:T(8,128)}, f32[192]{0:T(256)}) custom-call(bf16[32,512]{1,0:T(8,128)(2,1)} %bitcast.2, s32[1,384]{1,0:T(1,128)} %bitcast.3, s32[384]{0:T(512)} %row_hbm.1, s32[384]{0:T(512)} %bag_hbm.1, s32[512]{0:T(512)} %hot_id_hbm.1, s32[512]{0:T(512)} %hot_bag_hbm.1, f32[64,2048]{1,0:T(8,128)} %table_hbm.1, ...), custom_call_target="tpu_custom_call" | custom-call | tf_op jit(solution)/shard_map/exchange/pallas_call | solution.py:330
  46.9 19.3 %write.1 = (f32[64,2048]{1,0:T(8,128)}, f32[2048]{0:T(1024)}, f32[64,192]{1,0:T(8,128)}, f32[192]{0:T(256)}) custom-call(f32[64,2048]{1,0:T(8,128)} %get-tuple-element.8.table, f32[2048]{0:T(1024)} %get-tuple-element.9.accum, f32[64,192]{1,0:T(8,128)} %get-tuple-element.10.hot_table, f32[192]{0:T(256)} %get-tuple-element.11.hot_accum), custom_call_target="tpu_custom_call" | custom-call | tf_op jit(solution)/shard_map/write/pallas_call | solution.py:384

commit v4 on v3

--- a/solution.py
+++ b/solution.py
@@ -81,6 +81,7 @@
     hot_y_recv,
     hot_all_recv,
     square_recv,
+    hot_square_recv,
     fetch_sems,
     store_sems,
     send_sems,
@@ -104,7 +105,7 @@
         return other, {"row": other * NY + y, "col": col}
 
     def start(stage, count, along, me, send, recv):
-        for k in range(1, count):
+        for k in sorted(range(1, count), key=lambda k: -min(k, count - k)):
             other, device = along(k)
             pltpu.make_async_remote_copy(
                 src_ref=send.at[me if send is recv else other],
@@ -155,13 +156,32 @@
     pl.semaphore_wait(barrier, NC + NY + NZ - 3)
     start(0, NC, along_col, col, bags_send, bags_recv)
 
+    def place_of_bag(bag):
+        return ((bag >> 4) & 1) * 128 + (bag >> 5) * 16 + (bag & 15)
+
     for fetch in fetches[1:6]:
         fetch.wait()
+    hot_id = hot_id_ref[...].reshape(1, LH)
+    hot_line = (hot_id >> 4) * 8 + (hot_id & 7) + ((hot_id >> 3) & 1) * (NZ * 8)
+    hot_rows = one_hot(iota((NZ * 16, LH), 0) == hot_line)
+    hot_place = place_of_bag(hot_bag_ref[...].reshape(1, LH))
+    counts = dot_t(hot_rows, one_hot(iota((256, LH), 0) == hot_place))
+    counts = jnp.concatenate([counts[: NZ * 8], counts[NZ * 8 :]], axis=1)
+    count_high = counts.astype(BF16)
+    count_low = (counts - count_high.astype(F32)).astype(BF16)
+
     owner = owner_ref[...].reshape(1, LK)
     target = iota((NY * NZ, LK), 0) == owner
-    earlier = one_hot(iota((LK, LK), 0) < iota((LK, LK), 1))
-    before = dot(one_hot(target), earlier)
-    rank = jnp.sum(jnp.where(target, before, 0.0), axis=0, keepdims=True).astype(jnp.int32)
+    taken = one_hot(target)
+    earlier = one_hot(iota((128, 128), 0) < iota((128, 128), 1))
+    carry = jnp.zeros((NY * NZ, 1), F32)
+    ranks = []
+    for part in range(LK // 128):
+        at = slice(128 * part, 128 * part + 128)
+        before = dot(taken[:, at], earlier) + carry
+        ranks.append(jnp.sum(jnp.where(target[:, at], before, 0.0), axis=0, keepdims=True))
+        carry += jnp.sum(jnp.where(target[:, at], 1.0, 0.0), axis=1, keepdims=True)
+    rank = jnp.concatenate(ranks, axis=1).astype(jnp.int32)
     owner_z, owner_y = owner >> 3, owner & 7
     half, quarter = rank >> 2, rank & 3
     table_row = row_ref[...].reshape(1, LK)
@@ -176,27 +196,16 @@
     rows_y_recv[y] = rows_y_send[y]
     start(1, NY, along_y, y, rows_y_send, rows_y_recv)
 
-    def place_of_bag(bag):
-        return ((bag >> 4) & 1) * 128 + (bag >> 5) * 16 + (bag & 15)
-
-    position = owner_y * (NZ * 4) + owner_z * 4 + quarter + half * LK
-    placed = one_hot(iota((2 * LK, LK), 0) == position)
+    spot = one_hot(iota((NY * NZ, LK), 0) == half * (NZ * 4) + owner_z * 4 + quarter)
     cold_place = place_of_bag(bag_ref[...].reshape(1, LK)) + 1
-    cold_place = jnp.broadcast_to(cold_place, (8, LK)).astype(F32).astype(BF16)
-    slot_place = dot_t(placed, cold_place)[:, 0:1].astype(jnp.int32)
-    bag_number = iota((LK, 256), 1) + 1
-    pick = jnp.concatenate(
-        [one_hot(slot_place[:LK] == bag_number), one_hot(slot_place[LK:] == bag_number)], axis=1
-    )
-
-    hot_id = hot_id_ref[...].reshape(1, LH)
-    hot_line = (hot_id >> 4) * 8 + (hot_id & 7) + ((hot_id >> 3) & 1) * (NZ * 8)
-    hot_rows = one_hot(iota((NZ * 16, LH), 0) == hot_line)
-    hot_place = place_of_bag(hot_bag_ref[...].reshape(1, LH))
-    counts = dot_t(hot_rows, one_hot(iota((256, LH), 0) == hot_place))
-    counts = jnp.concatenate([counts[: NZ * 8], counts[NZ * 8 :]], axis=1)
-    count_high = counts.astype(BF16)
-    count_low = (counts - count_high.astype(F32)).astype(BF16)
+    weight = jnp.where(iota((NY, LK), 0) == owner_y, cold_place, 0).astype(F32).astype(BF16)
+    slot_place = dot_t(spot, weight).astype(jnp.int32)
+    bag_number = iota((NY * NZ, 256), 1) + 1
+    picks = []
+    for other in range(NY):
+        pick = jnp.where(slot_place[:, other : other + 1] == bag_number, 1.0, 0.0)
+        picks.append(jnp.concatenate([pick[: NZ * 4], pick[NZ * 4 :]], axis=1))
+    pick = jnp.concatenate(picks, axis=0).astype(BF16)
 
     wait(recv_sems.at[0], NC, bags_recv)
     bags = bags_recv[...].reshape(128, 128).astype(F32)
@@ -211,12 +220,12 @@
         ],
         axis=0,
     ).astype(BF16)
+    hot_z_send[...] = (dot(count_high, spread) + dot(count_low, spread)).reshape(NZ, 8, 128)
+    hot_z_recv[z] = hot_z_send[z]
+    start(3, NZ, along_z, z, hot_z_send, hot_z_recv)
     cold_y_send[...] = dot(pick, spread).astype(BF16).reshape(NY, NZ * 4, 128)
     cold_y_recv[y] = cold_y_send[y]
     start(2, NY, along_y, y, cold_y_send, cold_y_recv)
-    hot_z_send[...] = (dot(count_high, spread) + dot(count_low, spread)).reshape(NZ, 8, 128)
-    hot_z_recv[z] = hot_z_send[z]
-    start(3, NZ, along_z, z, hot_z_send, hot_z_recv)
 
     wait(recv_sems.at[1], NY, rows_y_recv)
     merged = jnp.sum(rows_y_recv[...], axis=0)
@@ -230,15 +239,15 @@
     source = ((out_row >> 2) & 7) * (NZ * 4) + (out_row >> 5) * 4 + (out_row & 3)
     regroup = one_hot(iota((LK, LK), 1) == source)
 
+    wait(recv_sems.at[3], NZ, hot_z_recv)
+    hot_y_recv[y] = jnp.sum(hot_z_recv[...], axis=0)
+    start(6, NY, along_y, y, hot_y_recv, hot_y_recv)
+
     wait(recv_sems.at[2], NY, cold_y_recv)
     regrouped = dot(regroup, cold_y_recv[...].reshape(LK, 128)).astype(BF16)
     cold_z_send[...] = regrouped.reshape(NZ, 32, 128)
     cold_z_recv[z] = cold_z_send[z]
     start(5, NZ, along_z, z, cold_z_send, cold_z_recv)
-
-    wait(recv_sems.at[3], NZ, hot_z_recv)
-    hot_y_recv[y] = jnp.sum(hot_z_recv[...], axis=0)
-    start(6, NY, along_y, y, hot_y_recv, hot_y_recv)
 
     wait(recv_sems.at[4], NZ, rows_z_recv)
     code = jnp.concatenate(
@@ -266,7 +275,8 @@
         part = grads[64 * h : 64 * h + 64]
         grad_ref[:, 256 * h : 256 * h + 256] = part
         squares.append(jnp.sum(part * part, axis=0, keepdims=True))
-    square_recv[col, :, 0:256] = jnp.concatenate(squares, axis=0)
+    square_recv[col] = jnp.concatenate(squares, axis=0)
+    start(8, NC, along_col, col, square_recv, square_recv)
 
     wait(recv_sems.at[7], NZ, hot_all_recv)
     pieces = []
@@ -275,16 +285,13 @@
         pieces += [piece, pltpu.roll(piece, 64, 1)]
     hot_grad = jnp.concatenate(pieces + [jnp.zeros((64, 128), F32)], axis=0).T[0:64]
     hot_squares = jnp.sum(hot_grad * hot_grad, axis=0, keepdims=True)
-    square_recv[col, :, 256:384] = jnp.concatenate(
+    hot_square_recv[col] = jnp.concatenate(
         [hot_squares[:, 0:128], hot_squares[:, 128:256], jnp.zeros((6, 128), F32)], axis=0
     )
-    start(8, NC, along_col, col, square_recv, square_recv)
+    start(9, NC, along_col, col, hot_square_recv, hot_square_recv)
     for fetch in fetches[6:]:
         fetch.wait()
-    wait(recv_sems.at[8], NC, square_recv)
-    total = square_recv[0]
-    for other in range(1, NC):
-        total += square_recv[other]
+
     stores = []
 
     def store(source, target):
@@ -292,15 +299,17 @@
         copy.start()
         stores.append(copy)
 
-    hot_total = jnp.concatenate([total[0:1, 256:384], total[1:2, 256:320]], axis=1)
-    accum = hot_accum_ref[...].reshape(1, 192) + hot_total / E
-    new_hot_accum_ref[...] = accum.reshape(192)
-    store(new_hot_accum_ref, new_hot_accum_hbm)
-    new_hot_ref[...] = hot_table_ref[...] - hot_grad[:, 0:192] * (LR / (jnp.sqrt(accum) + EPS))
-    store(new_hot_ref, new_hot_hbm)
+    def summed(ref):
+        total = ref[0]
+        for other in range(1, NC):
+            total += ref[other]
+        return total
+
+    wait(recv_sems.at[8], NC, square_recv)
+    total = summed(square_recv)
     for h in range(8):
         at = slice(256 * h, 256 * h + 256)
-        accum = accum_ref[at].reshape(1, 256) + total[h : h + 1, 0:256] / E
+        accum = accum_ref[at].reshape(1, 256) + total[h : h + 1] / E
         new_accum_ref[at] = accum.reshape(256)
         scale = LR / (jnp.sqrt(accum) + EPS)
         new_ref[:, at] = table_ref[:, at] - grad_ref[:, at] * scale
@@ -308,6 +317,15 @@
             done = slice(256 * h - 256, 256 * h + 256)
             store(new_ref.at[:, done], new_hbm.at[:, done])
     store(new_accum_ref, new_accum_hbm)
+
+    wait(recv_sems.at[9], NC, hot_square_recv)
+    total = summed(hot_square_recv)
+    hot_total = jnp.concatenate([total[0:1], total[1:2, 0:64]], axis=1)
+    accum = hot_accum_ref[...].reshape(1, 192) + hot_total / E
+    new_hot_accum_ref[...] = accum.reshape(192)
+    store(new_hot_accum_ref, new_hot_accum_hbm)
+    new_hot_ref[...] = hot_table_ref[...] - hot_grad[:, 0:192] * (LR / (jnp.sqrt(accum) + EPS))
+    store(new_hot_ref, new_hot_hbm)
 
     for stage, count, send in (
         (0, NC, bags_send),
@@ -319,6 +337,7 @@
         (6, NY, hot_y_recv),
         (7, NZ, hot_all_recv),
         (8, NC, square_recv),
+        (9, NC, hot_square_recv),
     ):
         wait(send_sems.at[stage], count, send)
     for copy in stores:
@@ -350,11 +369,12 @@
             pltpu.VMEM((NZ, 8, 128), F32),
             pltpu.VMEM((NY, 8, 128), F32),
             pltpu.VMEM((NZ, 8, 128), F32),
-            pltpu.VMEM((NC, 8, 384), F32),
+            pltpu.VMEM((NC, 8, 256), F32),
+            pltpu.VMEM((NC, 8, 128), F32),
             pltpu.SemaphoreType.DMA((10,)),
             pltpu.SemaphoreType.DMA((7,)),
-            pltpu.SemaphoreType.DMA((9,)),
-            pltpu.SemaphoreType.DMA((9,)),
+            pltpu.SemaphoreType.DMA((10,)),
+            pltpu.SemaphoreType.DMA((10,)),
         ],
         compiler_params=pltpu.CompilerParams(
             collective_id=0, has_side_effects=True, vmem_limit_bytes=60 * 1024 * 1024
@@ -363,20 +383,22 @@
     )(*operands)
 
 
-def write_kernel(table, accum, hot_table, hot_accum, *refs):
-    sems = refs[4]
-    copies = [
-        (table.at[0:32], refs[0].at[0:32]),
-        (table.at[32:64], refs[0].at[32:64]),
-        (accum, refs[1]),
-        (hot_table, refs[2]),
-        (hot_accum, refs[3]),
-    ]
-    copies = [pltpu.make_async_copy(*pair, sems.at[i]) for i, pair in enumerate(copies)]
-    for copy in copies:
-        copy.start()
-    for copy in copies:
-        copy.wait()
+def write_kernel(*refs):
+    sources, targets, holds, sems = refs[0:4], refs[4:8], refs[8:12], refs[12]
+    rows = sources[0].shape[0] // 4
+    parts = [(0, pl.ds(rows * part, rows)) for part in range(4)]
+    parts += [(i, slice(None)) for i in range(1, 4)]
+    loads, stores = [], []
+    for n, (i, at) in enumerate(parts):
+        loads.append(pltpu.make_async_copy(sources[i].at[at], holds[i].at[at], sems.at[0, n]))
+        stores.append(pltpu.make_async_copy(holds[i].at[at], targets[i].at[at], sems.at[1, n]))
+    for load in loads:
+        load.start()
+    for load, store in zip(loads, stores):
+        load.wait()
+        store.start()
+    for store in stores:
+        store.wait()
 
 
 def write(*arrays):
@@ -386,7 +408,10 @@
         out_shape=tuple(jax.ShapeDtypeStruct(a.shape, a.dtype) for a in arrays),
         in_specs=[hbm] * 4,
         out_specs=(hbm,) * 4,
-        scratch_shapes=[pltpu.SemaphoreType.DMA((5,))],
+        scratch_shapes=[
+            *(pltpu.VMEM(a.shape, a.dtype) for a in arrays),
+            pltpu.SemaphoreType.DMA((2, 7)),
+        ],
         compiler_params=pltpu.CompilerParams(vmem_limit_bytes=60 * 1024 * 1024),
         name="write",
     )(*arrays)

time: 66.4 us -> 47.1 us (0.71)
  Pallas kernels: 65.6 us -> 46.3 us
    pallas_call x1, Pallas kernels: 19.3 us -> 1.9 us  [write(): pl.pallas_call(write_kernel, out_shape=tuple((jax.ShapeDtypeStruct(a.shap...]
    pallas_call x1, Pallas kernels: 46.3 us -> 44.4 us  [exchange(): pl.pallas_call(exchange_kernel, out_shape=tuple((jax.ShapeDtypeStruct(a.s...]
where the time goes in v4:
time: 47.1 us; the launch traced here: 46.9 us
  Pallas kernels  46.3 us (98%)
  between operations  0.64 us (1%)
    pallas_call x1, Pallas kernels, exchange(): pl.pallas_call(exchange_kernel, out_shape=tuple((jax.ShapeDtypeStruct(a.s...  44.4 us
    pallas_call x1, Pallas kernels, write(): pl.pallas_call(write_kernel, out_shape=tuple((jax.ShapeDtypeStruct(a.shap...  1.9 us

profile of v4, /device:TPU:1, one launch (start us, length us, event | category | flops | bytes accessed | tf_op | source)
XLA Modules:
  0.0 46.9 jit_solution(6094272572419280533)
XLA Ops:
  0.6 44.4 %exchange.1 = (f32[64,2048]{1,0:T(8,128)}, f32[2048]{0:T(1024)}, f32[64,192]{1,0:T(8,128)}, f32[192]{0:T(256)}) custom-call(bf16[32,512]{1,0:T(8,128)(2,1)} %bitcast.2, s32[1,384]{1,0:T(1,128)} %bitcast.3, s32[384]{0:T(512)} %row_hbm.1, s32[384]{0:T(512)} %bag_hbm.1, s32[512]{0:T(512)} %hot_id_hbm.1, s32[512]{0:T(512)} %hot_bag_hbm.1, f32[64,2048]{1,0:T(8,128)} %table_hbm.1, ...), custom_call_target="tpu_custom_call" | custom-call | tf_op jit(solution)/shard_map/exchange/pallas_call | solution.py:349
  45.0 1.9 %write.1 = (f32[64,2048]{1,0:T(8,128)}, f32[2048]{0:T(1024)}, f32[64,192]{1,0:T(8,128)}, f32[192]{0:T(256)}) custom-call(f32[64,2048]{1,0:T(8,128)} %get-tuple-element.8.refs_0_, f32[2048]{0:T(1024)} %get-tuple-element.9.refs_1_, f32[64,192]{1,0:T(8,128)} %get-tuple-element.10.refs_2_, f32[192]{0:T(256)} %get-tuple-element.11.refs_3_), custom_call_target="tpu_custom_call" | custom-call | tf_op jit(solution)/shard_map/write/pallas_call | solution.py:406

commit v5 on v4

--- a/solution.py
+++ b/solution.py
@@ -72,16 +72,15 @@
     rows_y_recv,
     rows_z_send,
     rows_z_recv,
-    cold_y_send,
-    cold_y_recv,
-    cold_z_send,
-    cold_z_recv,
+    cold_send,
+    cold_recv,
     hot_z_send,
     hot_z_recv,
     hot_y_recv,
     hot_all_recv,
     square_recv,
     hot_square_recv,
+    hot_total_recv,
     fetch_sems,
     store_sems,
     send_sems,
@@ -119,11 +118,6 @@
     def wait(sem, count, ref):
         part = ref.at[pl.ds(0, count - 1)]
         pltpu.make_async_copy(part, part, sem).wait()
-
-    barrier = pltpu.get_barrier_semaphore()
-    for count, along in ((NC, along_col), (NY, along_y), (NZ, along_z)):
-        for k in range(1, count):
-            pl.semaphore_signal(barrier, inc=1, device_id=along(k)[1], device_id_type=MESH)
 
     fetches = [
         pltpu.make_async_copy(source, target, fetch_sems.at[i])
@@ -144,6 +138,26 @@
     ]
     for fetch in fetches:
         fetch.start()
+    barrier = pltpu.get_barrier_semaphore()
+    for count, along in ((NC, along_col), (NY, along_y), (NZ, along_z)):
+        for k in range(1, count):
+            pl.semaphore_signal(barrier, inc=1, device_id=along(k)[1], device_id_type=MESH)
+
+    def around(step_z, step_y):
+        other = lax.rem(z + step_z, NZ) * NY + lax.rem(y + step_y, NY)
+        return other, {"row": other, "col": col}
+
+    def all_of_row(act):
+        def ring(i, carry):
+            step_z = NZ // 2 + (1 - 2 * lax.rem(i, 2)) * lax.div(i + 1, 2)
+            for step_y in (4, 3, 5, 2, 6, 1, 7, 0):
+                act(*around(step_z, step_y))
+            return carry
+
+        lax.fori_loop(0, NZ - 1, ring, 0)
+        for step_y in (4, 3, 5, 2, 6, 1, 7):
+            act(*around(0, step_y))
+
     fetches[0].wait()
 
     low_lanes = iota((16, 128), 1) < 64
@@ -169,6 +183,7 @@
     counts = jnp.concatenate([counts[: NZ * 8], counts[NZ * 8 :]], axis=1)
     count_high = counts.astype(BF16)
     count_low = (counts - count_high.astype(F32)).astype(BF16)
+    count_parts = jnp.concatenate([count_high, count_low], axis=0)
 
     owner = owner_ref[...].reshape(1, LK)
     target = iota((NY * NZ, LK), 0) == owner
@@ -196,17 +211,6 @@
     rows_y_recv[y] = rows_y_send[y]
     start(1, NY, along_y, y, rows_y_send, rows_y_recv)
 
-    spot = one_hot(iota((NY * NZ, LK), 0) == half * (NZ * 4) + owner_z * 4 + quarter)
-    cold_place = place_of_bag(bag_ref[...].reshape(1, LK)) + 1
-    weight = jnp.where(iota((NY, LK), 0) == owner_y, cold_place, 0).astype(F32).astype(BF16)
-    slot_place = dot_t(spot, weight).astype(jnp.int32)
-    bag_number = iota((NY * NZ, 256), 1) + 1
-    picks = []
-    for other in range(NY):
-        pick = jnp.where(slot_place[:, other : other + 1] == bag_number, 1.0, 0.0)
-        picks.append(jnp.concatenate([pick[: NZ * 4], pick[NZ * 4 :]], axis=1))
-    pick = jnp.concatenate(picks, axis=0).astype(BF16)
-
     wait(recv_sems.at[0], NC, bags_recv)
     bags = bags_recv[...].reshape(128, 128).astype(F32)
     rolled = pltpu.roll(bags, 64, 1)
@@ -220,12 +224,10 @@
         ],
         axis=0,
     ).astype(BF16)
-    hot_z_send[...] = (dot(count_high, spread) + dot(count_low, spread)).reshape(NZ, 8, 128)
+    hot_parts = dot(count_parts, spread)
+    hot_z_send[...] = (hot_parts[: NZ * 8] + hot_parts[NZ * 8 :]).reshape(NZ, 8, 128)
     hot_z_recv[z] = hot_z_send[z]
     start(3, NZ, along_z, z, hot_z_send, hot_z_recv)
-    cold_y_send[...] = dot(pick, spread).astype(BF16).reshape(NY, NZ * 4, 128)
-    cold_y_recv[y] = cold_y_send[y]
-    start(2, NY, along_y, y, cold_y_send, cold_y_recv)
 
     wait(recv_sems.at[1], NY, rows_y_recv)
     merged = jnp.sum(rows_y_recv[...], axis=0)
@@ -235,19 +237,34 @@
     rows_z_recv[z] = rows_z_send[z]
     start(4, NZ, along_z, z, rows_z_send, rows_z_recv)
 
-    out_row = iota((LK, LK), 0)
-    source = ((out_row >> 2) & 7) * (NZ * 4) + (out_row >> 5) * 4 + (out_row & 3)
-    regroup = one_hot(iota((LK, LK), 1) == source)
+    spot = one_hot(iota((NY * CAP, LK), 0) == half * (NY * 4) + owner_y * 4 + quarter)
+    cold_place = place_of_bag(bag_ref[...].reshape(1, LK)) + 1
+    weight = jnp.where(iota((16, LK), 0) == owner_z, cold_place, 0).astype(F32).astype(BF16)
+    slot_place = dot_t(spot, weight).astype(jnp.int32)
+    bag_number = iota((NY * CAP, 256), 1) + 1
+    picks = []
+    for other in range(NZ):
+        pick = jnp.where(slot_place[:, other : other + 1] == bag_number, 1.0, 0.0)
+        picks.append(jnp.concatenate([pick[: NY * 4], pick[NY * 4 :]], axis=1))
+    pick = jnp.concatenate(picks, axis=0).astype(BF16)
+    cold_send[...] = dot(pick, spread).reshape(NY * NZ, 4, 128).astype(BF16)
+    cold_recv[row] = cold_send[row]
+
+    def send_cold(other, device):
+        pltpu.make_async_remote_copy(
+            src_ref=cold_send.at[other],
+            dst_ref=cold_recv.at[row],
+            send_sem=send_sems.at[2],
+            recv_sem=recv_sems.at[2],
+            device_id=device,
+            device_id_type=MESH,
+        ).start()
+
+    all_of_row(send_cold)
 
     wait(recv_sems.at[3], NZ, hot_z_recv)
     hot_y_recv[y] = jnp.sum(hot_z_recv[...], axis=0)
     start(6, NY, along_y, y, hot_y_recv, hot_y_recv)
-
-    wait(recv_sems.at[2], NY, cold_y_recv)
-    regrouped = dot(regroup, cold_y_recv[...].reshape(LK, 128)).astype(BF16)
-    cold_z_send[...] = regrouped.reshape(NZ, 32, 128)
-    cold_z_recv[z] = cold_z_send[z]
-    start(5, NZ, along_z, z, cold_z_send, cold_z_recv)
 
     wait(recv_sems.at[4], NZ, rows_z_recv)
     code = jnp.concatenate(
@@ -258,11 +275,14 @@
     land = [one_hot(code_low[side : side + 1] == low_number) for side in range(2)]
 
     wait(recv_sems.at[6], NY, hot_y_recv)
-    hot_all_recv[z] = jnp.sum(hot_y_recv[...], axis=0)
+    hot_mine = jnp.sum(hot_y_recv[...], axis=0)
+    hot_square_recv[col] = hot_mine * hot_mine
+    start(9, NC, along_col, col, hot_square_recv, hot_square_recv)
+    hot_all_recv[z] = hot_mine
     start(7, NZ, along_z, z, hot_all_recv, hot_all_recv)
 
-    wait(recv_sems.at[5], NZ, cold_z_recv)
-    arrived = cold_z_recv[...].reshape(LK, 128).astype(F32).T
+    wait(recv_sems.at[2], NY * NZ, cold_recv)
+    arrived = cold_recv[...].astype(F32).reshape(LK, 128).T
     grads = jnp.zeros((512, 256), F32)
     for side in range(2):
         mine = arrived[64 * side : 64 * side + 64]
@@ -278,32 +298,31 @@
     square_recv[col] = jnp.concatenate(squares, axis=0)
     start(8, NC, along_col, col, square_recv, square_recv)
 
-    wait(recv_sems.at[7], NZ, hot_all_recv)
-    pieces = []
-    for other in range(NZ):
-        piece = hot_all_recv[other]
-        pieces += [piece, pltpu.roll(piece, 64, 1)]
-    hot_grad = jnp.concatenate(pieces + [jnp.zeros((64, 128), F32)], axis=0).T[0:64]
-    hot_squares = jnp.sum(hot_grad * hot_grad, axis=0, keepdims=True)
-    hot_square_recv[col] = jnp.concatenate(
-        [hot_squares[:, 0:128], hot_squares[:, 128:256], jnp.zeros((6, 128), F32)], axis=0
-    )
-    start(9, NC, along_col, col, hot_square_recv, hot_square_recv)
-    for fetch in fetches[6:]:
-        fetch.wait()
-
-    stores = []
-
-    def store(source, target):
-        copy = pltpu.make_async_copy(source, target, store_sems.at[len(stores)])
-        copy.start()
-        stores.append(copy)
-
     def summed(ref):
         total = ref[0]
         for other in range(1, NC):
             total += ref[other]
         return total
+
+    wait(recv_sems.at[9], NC, hot_square_recv)
+    total = summed(hot_square_recv)
+    sub, at_lane = iota((8, 128), 0), iota((8, 128), 1)
+    first = jnp.sum(jnp.where(at_lane < 64, total, 0.0), axis=1, keepdims=True)
+    second = jnp.sum(jnp.where(at_lane < 64, 0.0, total), axis=1, keepdims=True)
+    both = jnp.where(((at_lane >> 3) & 1) == 0, first, second)
+    here = ((at_lane & 7) == sub) & ((at_lane >> 4) == lax.rem(z, 8))
+    hot_total_recv[z] = jnp.sum(jnp.where(here, both, 0.0), axis=0, keepdims=True)
+    start(5, NZ, along_z, z, hot_total_recv, hot_total_recv)
+
+    for fetch in fetches[6:]:
+        fetch.wait()
+
+    stores = []
+
+    def store(source, target):
+        copy = pltpu.make_async_copy(source, target, store_sems.at[len(stores)])
+        copy.start()
+        stores.append(copy)
 
     wait(recv_sems.at[8], NC, square_recv)
     total = summed(square_recv)
@@ -318,9 +337,17 @@
             store(new_ref.at[:, done], new_hbm.at[:, done])
     store(new_accum_ref, new_accum_hbm)
 
-    wait(recv_sems.at[9], NC, hot_square_recv)
-    total = summed(hot_square_recv)
-    hot_total = jnp.concatenate([total[0:1], total[1:2, 0:64]], axis=1)
+    wait(recv_sems.at[7], NZ, hot_all_recv)
+    pieces = []
+    for other in range(NZ):
+        piece = hot_all_recv[other]
+        pieces += [piece, pltpu.roll(piece, 64, 1)]
+    hot_grad = jnp.concatenate(pieces + [jnp.zeros((64, 128), F32)], axis=0).T[0:64]
+    wait(recv_sems.at[5], NZ, hot_total_recv)
+    hot_total = jnp.concatenate(
+        [jnp.sum(hot_total_recv[0:8], axis=0), jnp.sum(hot_total_recv[8:12], axis=0)[:, 0:64]],
+        axis=1,
+    )
     accum = hot_accum_ref[...].reshape(1, 192) + hot_total / E
     new_hot_accum_ref[...] = accum.reshape(192)
     store(new_hot_accum_ref, new_hot_accum_hbm)
@@ -330,10 +357,10 @@
     for stage, count, send in (
         (0, NC, bags_send),
         (1, NY, rows_y_send),
-        (2, NY, cold_y_send),
+        (2, NY * NZ, cold_send),
         (3, NZ, hot_z_send),
         (4, NZ, rows_z_send),
-        (5, NZ, cold_z_send),
+        (5, NZ, hot_total_recv),
         (6, NY, hot_y_recv),
         (7, NZ, hot_all_recv),
         (8, NC, square_recv),
@@ -361,16 +388,15 @@
             pltpu.VMEM((NY, 2 * NZ, 128), F32),
             pltpu.VMEM((NZ, 8, 128), F32),
             pltpu.VMEM((NZ, 8, 128), F32),
-            pltpu.VMEM((NY, NZ * 4, 128), BF16),
-            pltpu.VMEM((NY, NZ * 4, 128), BF16),
-            pltpu.VMEM((NZ, 32, 128), BF16),
-            pltpu.VMEM((NZ, 32, 128), BF16),
+            pltpu.VMEM((NY * NZ, 4, 128), BF16),
+            pltpu.VMEM((NY * NZ, 4, 128), BF16),
             pltpu.VMEM((NZ, 8, 128), F32),
             pltpu.VMEM((NZ, 8, 128), F32),
             pltpu.VMEM((NY, 8, 128), F32),
             pltpu.VMEM((NZ, 8, 128), F32),
             pltpu.VMEM((NC, 8, 256), F32),
             pltpu.VMEM((NC, 8, 128), F32),
+            pltpu.VMEM((NZ, 1, 128), F32),
             pltpu.SemaphoreType.DMA((10,)),
             pltpu.SemaphoreType.DMA((7,)),
             pltpu.SemaphoreType.DMA((10,)),

time: 47.1 us -> 46 us (0.977)
  Pallas kernels: 46.3 us -> 45.2 us
    pallas_call x1, Pallas kernels: 44.4 us -> 43.3 us  [exchange(): pl.pallas_call(exchange_kernel, out_shape=tuple((jax.ShapeDtypeStruct(a.s...]
where the time goes in v5:
time: 46 us; the launch traced here: 45.8 us
  Pallas kernels  45.2 us (98%)
  between operations  0.64 us (1%)
    pallas_call x1, Pallas kernels, exchange(): pl.pallas_call(exchange_kernel, out_shape=tuple((jax.ShapeDtypeStruct(a.s...  43.3 us
    pallas_call x1, Pallas kernels, write(): pl.pallas_call(write_kernel, out_shape=tuple((jax.ShapeDtypeStruct(a.shap...  1.9 us

profile of v5, /device:TPU:1, one launch (start us, length us, event | category | flops | bytes accessed | tf_op | source)
XLA Modules:
  0.0 45.8 jit_solution(917561814260727799)
XLA Ops:
  0.6 43.3 %exchange.1 = (f32[64,2048]{1,0:T(8,128)}, f32[2048]{0:T(1024)}, f32[64,192]{1,0:T(8,128)}, f32[192]{0:T(256)}) custom-call(bf16[32,512]{1,0:T(8,128)(2,1)} %bitcast.2, s32[1,384]{1,0:T(1,128)} %bitcast.3, s32[384]{0:T(512)} %row_hbm.1, s32[384]{0:T(512)} %bag_hbm.1, s32[512]{0:T(512)} %hot_id_hbm.1, s32[512]{0:T(512)} %hot_bag_hbm.1, f32[64,2048]{1,0:T(8,128)} %table_hbm.1, ...), custom_call_target="tpu_custom_call" | custom-call | tf_op jit(solution)/shard_map/exchange/pallas_call | solution.py:376
  43.9 1.9 %write.1 = (f32[64,2048]{1,0:T(8,128)}, f32[2048]{0:T(1024)}, f32[64,192]{1,0:T(8,128)}, f32[192]{0:T(256)}) custom-call(f32[64,2048]{1,0:T(8,128)} %get-tuple-element.8.refs_0_, f32[2048]{0:T(1024)} %get-tuple-element.9.refs_1_, f32[64,192]{1,0:T(8,128)} %get-tuple-element.10.refs_2_, f32[192]{0:T(256)} %get-tuple-element.11.refs_3_), custom_call_target="tpu_custom_call" | custom-call | tf_op jit(solution)/shard_map/write/pallas_call | solution.py:432

commit v6 on v5

--- a/solution.py
+++ b/solution.py
@@ -85,6 +85,7 @@
     store_sems,
     send_sems,
     recv_sems,
+    relay_sems,
 ):
     row = lax.axis_index("row")
     col = lax.axis_index("col")
@@ -139,24 +140,27 @@
     for fetch in fetches:
         fetch.start()
     barrier = pltpu.get_barrier_semaphore()
-    for count, along in ((NC, along_col), (NY, along_y), (NZ, along_z)):
-        for k in range(1, count):
-            pl.semaphore_signal(barrier, inc=1, device_id=along(k)[1], device_id_type=MESH)
+    near_z, near_y = NZ // 4, NY // 4
+    greeted = [along_col(k)[1] for k in range(1, NC)]
+    greeted += [along_z(k)[1] for k in range(1, near_z + 1)]
+    greeted += [along_z(NZ - k)[1] for k in range(1, near_z + 1)]
+    greeted += [along_y(k)[1] for k in range(1, near_y + 1)]
+    greeted += [along_y(NY - k)[1] for k in range(1, near_y + 1)]
+    for device in greeted:
+        pl.semaphore_signal(barrier, inc=1, device_id=device, device_id_type=MESH)
 
     def around(step_z, step_y):
         other = lax.rem(z + step_z, NZ) * NY + lax.rem(y + step_y, NY)
         return other, {"row": other, "col": col}
 
-    def all_of_row(act):
+    def rings(first, last, act):
         def ring(i, carry):
             step_z = NZ // 2 + (1 - 2 * lax.rem(i, 2)) * lax.div(i + 1, 2)
             for step_y in (4, 3, 5, 2, 6, 1, 7, 0):
                 act(*around(step_z, step_y))
             return carry
 
-        lax.fori_loop(0, NZ - 1, ring, 0)
-        for step_y in (4, 3, 5, 2, 6, 1, 7):
-            act(*around(0, step_y))
+        lax.fori_loop(first, last, ring, 0)
 
     fetches[0].wait()
 
@@ -167,8 +171,13 @@
         bags_send[2 * pair] = jnp.where(low_lanes, first, pltpu.roll(second, 64, 1)).astype(BF16)
         bags_send[2 * pair + 1] = jnp.where(low_lanes, pltpu.roll(first, 64, 1), second).astype(BF16)
     bags_recv[col] = bags_send[col]
-    pl.semaphore_wait(barrier, NC + NY + NZ - 3)
+    pl.semaphore_wait(barrier, len(greeted))
     start(0, NC, along_col, col, bags_send, bags_recv)
+    for i, (along, count, step) in enumerate(((along_z, NZ, near_z), (along_y, NY, near_y))):
+        for k in (step, count - step):
+            pl.semaphore_signal(
+                relay_sems.at[i], inc=1, device_id=along(k)[1], device_id_type=MESH
+            )
 
     def place_of_bag(bag):
         return ((bag >> 4) & 1) * 128 + (bag >> 5) * 16 + (bag & 15)
@@ -209,6 +218,8 @@
     codes = dot_t(in_line, high) * 256.0 + dot_t(in_line, low)
     rows_y_send[...] = codes.reshape(NY, 2 * NZ, 128)
     rows_y_recv[y] = rows_y_send[y]
+    pl.semaphore_wait(relay_sems.at[0], 2)
+    pl.semaphore_wait(relay_sems.at[1], 2)
     start(1, NY, along_y, y, rows_y_send, rows_y_recv)
 
     wait(recv_sems.at[0], NC, bags_recv)
@@ -260,11 +271,15 @@
             device_id_type=MESH,
         ).start()
 
-    all_of_row(send_cold)
+    rings(0, 7, send_cold)
 
     wait(recv_sems.at[3], NZ, hot_z_recv)
     hot_y_recv[y] = jnp.sum(hot_z_recv[...], axis=0)
     start(6, NY, along_y, y, hot_y_recv, hot_y_recv)
+
+    rings(7, NZ - 1, send_cold)
+    for step_y in (4, 3, 5, 2, 6, 1, 7):
+        send_cold(*around(0, step_y))
 
     wait(recv_sems.at[4], NZ, rows_z_recv)
     code = jnp.concatenate(
@@ -401,6 +416,7 @@
             pltpu.SemaphoreType.DMA((7,)),
             pltpu.SemaphoreType.DMA((10,)),
             pltpu.SemaphoreType.DMA((10,)),
+            pltpu.SemaphoreType.REGULAR((2,)),
         ],
         compiler_params=pltpu.CompilerParams(
             collective_id=0, has_side_effects=True, vmem_limit_bytes=60 * 1024 * 1024

time: 46 us -> 45.2 us (0.983)
  Pallas kernels: 45.2 us -> 44.3 us
    pallas_call x1, Pallas kernels: 43.3 us -> 42.4 us  [exchange(): pl.pallas_call(exchange_kernel, out_shape=tuple((jax.ShapeDtypeStruct(a.s...]
where the time goes in v6:
time: 45.2 us; the launch traced here: 45 us
  Pallas kernels  44.3 us (98%)
  between operations  0.64 us (1%)
    pallas_call x1, Pallas kernels, exchange(): pl.pallas_call(exchange_kernel, out_shape=tuple((jax.ShapeDtypeStruct(a.s...  42.4 us
    pallas_call x1, Pallas kernels, write(): pl.pallas_call(write_kernel, out_shape=tuple((jax.ShapeDtypeStruct(a.shap...  1.9 us

profile of v6, /device:TPU:1, one launch (start us, length us, event | category | flops | bytes accessed | tf_op | source)
XLA Modules:
  0.0 45.0 jit_solution(10063771694676865774)
XLA Ops:
  0.6 42.4 %exchange.1 = (f32[64,2048]{1,0:T(8,128)}, f32[2048]{0:T(1024)}, f32[64,192]{1,0:T(8,128)}, f32[192]{0:T(256)}) custom-call(bf16[32,512]{1,0:T(8,128)(2,1)} %bitcast.2, s32[1,384]{1,0:T(1,128)} %bitcast.3, s32[384]{0:T(512)} %row_hbm.1, s32[384]{0:T(512)} %bag_hbm.1, s32[512]{0:T(512)} %hot_id_hbm.1, s32[512]{0:T(512)} %hot_bag_hbm.1, f32[64,2048]{1,0:T(8,128)} %table_hbm.1, ...), custom_call_target="tpu_custom_call" | custom-call | tf_op jit(solution)/shard_map/exchange/pallas_call | solution.py:391
  43.1 1.9 %write.1 = (f32[64,2048]{1,0:T(8,128)}, f32[2048]{0:T(1024)}, f32[64,192]{1,0:T(8,128)}, f32[192]{0:T(256)}) custom-call(f32[64,2048]{1,0:T(8,128)} %get-tuple-element.8.refs_0_, f32[2048]{0:T(1024)} %get-tuple-element.9.refs_1_, f32[64,192]{1,0:T(8,128)} %get-tuple-element.10.refs_2_, f32[192]{0:T(256)} %get-tuple-element.11.refs_3_), custom_call_target="tpu_custom_call" | custom-call | tf_op jit(solution)/shard_map/write/pallas_call | solution.py:448

commit v7 on v6

--- a/solution.py
+++ b/solution.py
@@ -12,6 +12,7 @@
 
 NC = 8
 NY = 8
+NX = 4
 NZ = 12
 LK = 384
 LH = 512
@@ -66,6 +67,7 @@
     new_hot_ref,
     new_hot_accum_ref,
     grad_ref,
+    land_ref,
     bags_send,
     bags_recv,
     rows_y_send,
@@ -104,6 +106,10 @@
         other = lax.rem(z + k, NZ)
         return other, {"row": other * NY + y, "col": col}
 
+    def along_core(k):
+        other = col + k - 2 * lax.rem(col, 2)
+        return other, {"row": row, "col": other}
+
     def start(stage, count, along, me, send, recv):
         for k in sorted(range(1, count), key=lambda k: -min(k, count - k)):
             other, device = along(k)
@@ -137,17 +143,18 @@
             )
         )
     ]
-    for fetch in fetches:
-        fetch.start()
+    fetches[0].start()
     barrier = pltpu.get_barrier_semaphore()
     near_z, near_y = NZ // 4, NY // 4
-    greeted = [along_col(k)[1] for k in range(1, NC)]
-    greeted += [along_z(k)[1] for k in range(1, near_z + 1)]
-    greeted += [along_z(NZ - k)[1] for k in range(1, near_z + 1)]
-    greeted += [along_y(k)[1] for k in range(1, near_y + 1)]
-    greeted += [along_y(NY - k)[1] for k in range(1, near_y + 1)]
+    greeted = []
+    for along, count, near in ((along_z, NZ, near_z), (along_y, NY, near_y), (along_col, NC, NC // 2)):
+        steps = {k for step in range(1, near + 1) for k in (step, count - step)}
+        for k in sorted(steps, key=lambda k: -min(k, count - k)):
+            greeted.append(along(k)[1])
     for device in greeted:
         pl.semaphore_signal(barrier, inc=1, device_id=device, device_id_type=MESH)
+    for fetch in fetches[1:]:
+        fetch.start()
 
     def around(step_z, step_y):
         other = lax.rem(z + step_z, NZ) * NY + lax.rem(y + step_y, NY)
@@ -237,8 +244,8 @@
     ).astype(BF16)
     hot_parts = dot(count_parts, spread)
     hot_z_send[...] = (hot_parts[: NZ * 8] + hot_parts[NZ * 8 :]).reshape(NZ, 8, 128)
+    start(3, NZ, along_z, z, hot_z_send, hot_z_recv)
     hot_z_recv[z] = hot_z_send[z]
-    start(3, NZ, along_z, z, hot_z_send, hot_z_recv)
 
     wait(recv_sems.at[1], NY, rows_y_recv)
     merged = jnp.sum(rows_y_recv[...], axis=0)
@@ -287,24 +294,58 @@
     ).astype(jnp.int32)
     code_high, code_low = code >> 8, code & 255
     low_number = iota((256, LK), 0)
-    land = [one_hot(code_low[side : side + 1] == low_number) for side in range(2)]
+    land = jnp.concatenate(
+        [jnp.where(code_low[side : side + 1] == low_number, 1.0, 0.0).T for side in range(2)], axis=0
+    )
+    land_ref[...] = land.astype(BF16)
 
     wait(recv_sems.at[6], NY, hot_y_recv)
     hot_mine = jnp.sum(hot_y_recv[...], axis=0)
-    hot_square_recv[col] = hot_mine * hot_mine
-    start(9, NC, along_col, col, hot_square_recv, hot_square_recv)
+    core, chip_x = lax.rem(col, 2), lax.div(col, 2)
+    hot_square_recv[core] = hot_mine * hot_mine
+    start(9, 2, along_core, core, hot_square_recv, hot_square_recv)
     hot_all_recv[z] = hot_mine
     start(7, NZ, along_z, z, hot_all_recv, hot_all_recv)
 
+    wait(recv_sems.at[9], 2, hot_square_recv)
+    total = hot_square_recv[0] + hot_square_recv[1]
+    sub, at_lane = iota((8, 128), 0), iota((8, 128), 1)
+    first = jnp.sum(jnp.where(at_lane < 64, total, 0.0), axis=1, keepdims=True)
+    second = jnp.sum(jnp.where(at_lane < 64, 0.0, total), axis=1, keepdims=True)
+    both = jnp.where(((at_lane >> 3) & 1) == 0, first, second)
+    here = ((at_lane & 7) == sub) & ((at_lane >> 4) == lax.rem(z, 8))
+    mine_at = z * NX + chip_x
+    hot_total_recv[mine_at] = jnp.sum(jnp.where(here, both, 0.0), axis=0, keepdims=True)
+
+    def send_total(step_z, step_x):
+        device = {
+            "row": lax.rem(z + step_z, NZ) * NY + y,
+            "col": lax.rem(chip_x + step_x, NX) * 2 + core,
+        }
+        pltpu.make_async_remote_copy(
+            src_ref=hot_total_recv.at[mine_at],
+            dst_ref=hot_total_recv.at[mine_at],
+            send_sem=send_sems.at[5],
+            recv_sem=recv_sems.at[5],
+            device_id=device,
+            device_id_type=MESH,
+        ).start()
+
+    by_distance = sorted(
+        ((step_z, step_x) for step_z in range(NZ) for step_x in range(NX)),
+        key=lambda s: -(min(s[0], NZ - s[0]) + min(s[1], NX - s[1])),
+    )[:-1]
+    for steps in by_distance[:18]:
+        send_total(*steps)
+
     wait(recv_sems.at[2], NY * NZ, cold_recv)
     arrived = cold_recv[...].astype(F32).reshape(LK, 128).T
-    grads = jnp.zeros((512, 256), F32)
+    masked = []
     for side in range(2):
         mine = arrived[64 * side : 64 * side + 64]
-        masked = jnp.concatenate(
-            [jnp.where(code_high[side : side + 1] == h + 1, mine, 0.0) for h in range(8)], axis=0
-        ).astype(BF16)
-        grads += dot_t(masked, land[side])
+        blocks = [jnp.where(code_high[side : side + 1] == h + 1, mine, 0.0) for h in range(8)]
+        masked.append(jnp.concatenate(blocks, axis=0).astype(BF16))
+    grads = dot(jnp.concatenate(masked, axis=1), land_ref[...])
     squares = []
     for h in range(8):
         part = grads[64 * h : 64 * h + 64]
@@ -319,16 +360,8 @@
             total += ref[other]
         return total
 
-    wait(recv_sems.at[9], NC, hot_square_recv)
-    total = summed(hot_square_recv)
-    sub, at_lane = iota((8, 128), 0), iota((8, 128), 1)
-    first = jnp.sum(jnp.where(at_lane < 64, total, 0.0), axis=1, keepdims=True)
-    second = jnp.sum(jnp.where(at_lane < 64, 0.0, total), axis=1, keepdims=True)
-    both = jnp.where(((at_lane >> 3) & 1) == 0, first, second)
-    here = ((at_lane & 7) == sub) & ((at_lane >> 4) == lax.rem(z, 8))
-    hot_total_recv[z] = jnp.sum(jnp.where(here, both, 0.0), axis=0, keepdims=True)
-    start(5, NZ, along_z, z, hot_total_recv, hot_total_recv)
-
+    for steps in by_distance[18:]:
+        send_total(*steps)
     for fetch in fetches[6:]:
         fetch.wait()
 
@@ -358,9 +391,13 @@
         piece = hot_all_recv[other]
         pieces += [piece, pltpu.roll(piece, 64, 1)]
     hot_grad = jnp.concatenate(pieces + [jnp.zeros((64, 128), F32)], axis=0).T[0:64]
-    wait(recv_sems.at[5], NZ, hot_total_recv)
+    wait(recv_sems.at[5], NZ * NX, hot_total_recv)
+    split = 8 * NX
     hot_total = jnp.concatenate(
-        [jnp.sum(hot_total_recv[0:8], axis=0), jnp.sum(hot_total_recv[8:12], axis=0)[:, 0:64]],
+        [
+            jnp.sum(hot_total_recv[0:split], axis=0),
+            jnp.sum(hot_total_recv[split : NZ * NX], axis=0)[:, 0:64],
+        ],
         axis=1,
     )
     accum = hot_accum_ref[...].reshape(1, 192) + hot_total / E
@@ -375,11 +412,11 @@
         (2, NY * NZ, cold_send),
         (3, NZ, hot_z_send),
         (4, NZ, rows_z_send),
-        (5, NZ, hot_total_recv),
+        (5, NZ * NX, hot_total_recv),
         (6, NY, hot_y_recv),
         (7, NZ, hot_all_recv),
         (8, NC, square_recv),
-        (9, NC, hot_square_recv),
+        (9, 2, hot_square_recv),
     ):
         wait(send_sems.at[stage], count, send)
     for copy in stores:
@@ -397,6 +434,7 @@
             *(pltpu.VMEM(a.shape, a.dtype) for a in operands),
             *(pltpu.VMEM(a.shape, F32) for a in operands[6:]),
             pltpu.VMEM((64, 2048), F32),
+            pltpu.VMEM((2 * LK, 256), BF16),
             pltpu.VMEM((NC, 16, 128), BF16),
             pltpu.VMEM((NC, 16, 128), BF16),
             pltpu.VMEM((NY, 2 * NZ, 128), F32),
@@ -410,8 +448,8 @@
             pltpu.VMEM((NY, 8, 128), F32),
             pltpu.VMEM((NZ, 8, 128), F32),
             pltpu.VMEM((NC, 8, 256), F32),
-            pltpu.VMEM((NC, 8, 128), F32),
-            pltpu.VMEM((NZ, 1, 128), F32),
+            pltpu.VMEM((2, 8, 128), F32),
+            pltpu.VMEM((NZ * NX, 1, 128), F32),
             pltpu.SemaphoreType.DMA((10,)),
             pltpu.SemaphoreType.DMA((7,)),
             pltpu.SemaphoreType.DMA((10,)),

time: 45.2 us -> 44 us (0.973)
  Pallas kernels: 44.3 us -> 43.2 us
    pallas_call x1, Pallas kernels: 42.4 us -> 41.3 us  [exchange(): pl.pallas_call(exchange_kernel, out_shape=tuple((jax.ShapeDtypeStruct(a.s...]
where the time goes in v7:
time: 44 us; the launch traced here: 43.8 us
  Pallas kernels  43.2 us (98%)
  between operations  0.64 us (1%)
    pallas_call x1, Pallas kernels, exchange(): pl.pallas_call(exchange_kernel, out_shape=tuple((jax.ShapeDtypeStruct(a.s...  41.3 us
    pallas_call x1, Pallas kernels, write(): pl.pallas_call(write_kernel, out_shape=tuple((jax.ShapeDtypeStruct(a.shap...  1.9 us

profile of v7, /device:TPU:1, one launch (start us, length us, event | category | flops | bytes accessed | tf_op | source)
XLA Modules:
  0.0 43.8 jit_solution(15910897952733934090)
XLA Ops:
  0.6 41.3 %exchange.1 = (f32[64,2048]{1,0:T(8,128)}, f32[2048]{0:T(1024)}, f32[64,192]{1,0:T(8,128)}, f32[192]{0:T(256)}) custom-call(bf16[32,512]{1,0:T(8,128)(2,1)} %bitcast.2, s32[1,384]{1,0:T(1,128)} %bitcast.3, s32[384]{0:T(512)} %row_hbm.1, s32[384]{0:T(512)} %bag_hbm.1, s32[512]{0:T(512)} %hot_id_hbm.1, s32[512]{0:T(512)} %hot_bag_hbm.1, f32[64,2048]{1,0:T(8,128)} %table_hbm.1, ...), custom_call_target="tpu_custom_call" | custom-call | tf_op jit(solution)/shard_map/exchange/pallas_call | solution.py:428
  41.9 1.9 %write.1 = (f32[64,2048]{1,0:T(8,128)}, f32[2048]{0:T(1024)}, f32[64,192]{1,0:T(8,128)}, f32[192]{0:T(256)}) custom-call(f32[64,2048]{1,0:T(8,128)} %get-tuple-element.8.refs_0_, f32[2048]{0:T(1024)} %get-tuple-element.9.refs_1_, f32[64,192]{1,0:T(8,128)} %get-tuple-element.10.refs_2_, f32[192]{0:T(256)} %get-tuple-element.11.refs_3_), custom_call_target="tpu_custom_call" | custom-call | tf_op jit(solution)/shard_map/write/pallas_call | solution.py:486

commit v8 on v7

--- a/solution.py
+++ b/solution.py
@@ -229,6 +229,16 @@
     pl.semaphore_wait(relay_sems.at[1], 2)
     start(1, NY, along_y, y, rows_y_send, rows_y_recv)
 
+    spot = one_hot(iota((NY * CAP, LK), 0) == half * (NY * 4) + owner_y * 4 + quarter)
+    cold_place = place_of_bag(bag_ref[...].reshape(1, LK)) + 1
+    weight = jnp.where(iota((16, LK), 0) == owner_z, cold_place, 0).astype(F32).astype(BF16)
+    slot_place = dot_t(spot, weight).astype(jnp.int32)
+    bag_number = iota((NY * CAP, 256), 1) + 1
+    picks = []
+    for other in range(NZ):
+        pick = jnp.where(slot_place[:, other : other + 1] == bag_number, 1.0, 0.0)
+        picks.append(jnp.concatenate([pick[: NY * 4], pick[NY * 4 :]], axis=1))
+    pick = jnp.concatenate(picks, axis=0).astype(BF16)
     wait(recv_sems.at[0], NC, bags_recv)
     bags = bags_recv[...].reshape(128, 128).astype(F32)
     rolled = pltpu.roll(bags, 64, 1)
@@ -255,16 +265,6 @@
     rows_z_recv[z] = rows_z_send[z]
     start(4, NZ, along_z, z, rows_z_send, rows_z_recv)
 
-    spot = one_hot(iota((NY * CAP, LK), 0) == half * (NY * 4) + owner_y * 4 + quarter)
-    cold_place = place_of_bag(bag_ref[...].reshape(1, LK)) + 1
-    weight = jnp.where(iota((16, LK), 0) == owner_z, cold_place, 0).astype(F32).astype(BF16)
-    slot_place = dot_t(spot, weight).astype(jnp.int32)
-    bag_number = iota((NY * CAP, 256), 1) + 1
-    picks = []
-    for other in range(NZ):
-        pick = jnp.where(slot_place[:, other : other + 1] == bag_number, 1.0, 0.0)
-        picks.append(jnp.concatenate([pick[: NY * 4], pick[NY * 4 :]], axis=1))
-    pick = jnp.concatenate(picks, axis=0).astype(BF16)
     cold_send[...] = dot(pick, spread).reshape(NY * NZ, 4, 128).astype(BF16)
     cold_recv[row] = cold_send[row]
 

time: 44 us -> 44.3 us (level)
  no operation moved by 1% of the time
where the time goes in v8:
time: 44.3 us; the launch traced here: 44.1 us
  Pallas kernels  43.4 us (98%)
  between operations  0.64 us (1%)
    pallas_call x1, Pallas kernels, exchange(): pl.pallas_call(exchange_kernel, out_shape=tuple((jax.ShapeDtypeStruct(a.s...  41.5 us
    pallas_call x1, Pallas kernels, write(): pl.pallas_call(write_kernel, out_shape=tuple((jax.ShapeDtypeStruct(a.shap...  1.9 us

profile of v8, /device:TPU:1, one launch (start us, length us, event | category | flops | bytes accessed | tf_op | source)
XLA Modules:
  0.0 44.1 jit_solution(12242664186595741772)
XLA Ops:
  0.6 41.5 %exchange.1 = (f32[64,2048]{1,0:T(8,128)}, f32[2048]{0:T(1024)}, f32[64,192]{1,0:T(8,128)}, f32[192]{0:T(256)}) custom-call(bf16[32,512]{1,0:T(8,128)(2,1)} %bitcast.2, s32[1,384]{1,0:T(1,128)} %bitcast.3, s32[384]{0:T(512)} %row_hbm.1, s32[384]{0:T(512)} %bag_hbm.1, s32[512]{0:T(512)} %hot_id_hbm.1, s32[512]{0:T(512)} %hot_bag_hbm.1, f32[64,2048]{1,0:T(8,128)} %table_hbm.1, ...), custom_call_target="tpu_custom_call" | custom-call | tf_op jit(solution)/shard_map/exchange/pallas_call | solution.py:428
  42.2 1.9 %write.1 = (f32[64,2048]{1,0:T(8,128)}, f32[2048]{0:T(1024)}, f32[64,192]{1,0:T(8,128)}, f32[192]{0:T(256)}) custom-call(f32[64,2048]{1,0:T(8,128)} %get-tuple-element.8.refs_0_, f32[2048]{0:T(1024)} %get-tuple-element.9.refs_1_, f32[64,192]{1,0:T(8,128)} %get-tuple-element.10.refs_2_, f32[192]{0:T(256)} %get-tuple-element.11.refs_3_), custom_call_target="tpu_custom_call" | custom-call | tf_op jit(solution)/shard_map/write/pallas_call | solution.py:486
